TPU v7x, 512 devices: a whole 4x4x16 slice. The times are simulated.
512 devices in a mesh: blk: 32 (over z, y_lo), probe: 16 (over y_hi, x, core).
Axes of the slice: x: 4, y: 4 (y_hi: 2, y_lo: 2; y = y_hi * 2 + y_lo), z: 16, core: 2. Of those that a mesh axis runs over, the one named last changes fastest.
Arguments:
- points: bfloat16 [65536, 256], P(('blk', 'probe')), may hold values from -6 to 6, as said below
- inv_length: float32 [256], replicated, may hold values from 0.07 to 0.26
- solution: float32 [64, 65536], P('probe', 'blk'), may hold values from -6 to 6
- residual: float32 [64, 65536], P('probe', 'blk'), may hold values from -53 to 53, as said below
- direction: float32 [64, 65536], P('probe', 'blk'), may hold values from -53 to 53, as said below
Outputs:
- new_solution: float32 [64, 65536], P('probe', 'blk')
- new_residual: float32 [64, 65536], P('probe', 'blk')
- new_direction: float32 [64, 65536], P('probe', 'blk')
Inputs may be any that keep to these rules, and one draw needn't show every extreme that they name: real-valued points. `residual`: a real-valued field. `direction`: a real-valued field.
All inputs are finite; a program needn't handle non-finite values.
Results may differ from a plain program's by a relative error of at most 0.0065.
Values may be sent and summed in bfloat16 or wider, within the bound.
No kernel may reach another device: no remote copies, remote signals or barrier semaphores. Data moves between devices by JAX's collectives and lax.ppermute only.
A program may use at most 64 MiB of HBM per device.

v0:
```python
import jax
import jax.numpy as jnp
from jax import lax
from jax.sharding import PartitionSpec as P

noise_var = 0.1
epsilon = 1e-06


def shifted(shard, axis, by):
    devices = lax.axis_size(axis)
    return lax.ppermute(shard, axis, [(i, (i + by) % devices) for i in range(devices)])


def kernel_tile(row_pts, col_pts):
    row_norms = jnp.sum(jnp.square(row_pts.astype(jnp.float32)), axis=1)
    col_norms = jnp.sum(jnp.square(col_pts.astype(jnp.float32)), axis=1)
    inner = jnp.dot(row_pts, col_pts.T, preferred_element_type=jnp.float32)
    squared = jnp.maximum(row_norms[:, None] + col_norms[None, :] - 2.0 * inner, 0.0)
    distance = jnp.sqrt(5.0 * squared)
    return ((1.0 + distance + distance * distance / 3.0) * jnp.exp(-distance)).astype(jnp.bfloat16)


def shards(points, inv_length, solution, residual, direction):
    own_rows = (points.astype(jnp.float32) * inv_length[None, :]).astype(jnp.bfloat16)
    block_pts = lax.all_gather(own_rows, "probe", axis=0, tiled=True)
    low_direction = direction.astype(jnp.bfloat16)
    own_dir = lax.all_to_all(low_direction, "probe", split_axis=1, concat_axis=0, tiled=True)
    partial_value = jnp.dot(
        own_dir, kernel_tile(own_rows, block_pts), preferred_element_type=jnp.float32
    )
    cycle_size = lax.axis_size("blk")

    def advance(counter, loop_state):
        moving_pts, moving_dir, summed = loop_state
        moving_pts, moving_dir = shifted((moving_pts, moving_dir), "blk", 1)
        summed = summed + jnp.dot(
            moving_dir, kernel_tile(moving_pts, block_pts), preferred_element_type=jnp.float32
        )
        return (moving_pts, moving_dir, summed)

    spent_pts, spent_dir, partial_value = lax.fori_loop(
        0, cycle_size - 1, advance, (own_rows, own_dir, partial_value)
    )
    image = lax.psum_scatter(
        partial_value, "probe", scatter_dimension=0, tiled=True
    ) + noise_var * low_direction.astype(jnp.float32)
    old_norm = lax.psum(jnp.sum(residual * residual, axis=1), "blk")
    curvature = lax.psum(jnp.sum(direction * image, axis=1), "blk")
    step_len = old_norm / curvature
    new_residual = residual - step_len[:, None] * image
    new_norm = lax.psum(jnp.sum(new_residual * new_residual, axis=1), "blk")
    new_solution = solution + step_len[:, None] * direction
    new_direction = new_residual + (new_norm / (old_norm + epsilon))[:, None] * direction
    return (new_solution, new_residual, new_direction)


def solution(mesh):
    placed = (
        P(("blk", "probe"), None),
        P(),
        P("probe", "blk"),
        P("probe", "blk"),
        P("probe", "blk"),
    )
    return jax.shard_map(
        shards,
        mesh=mesh,
        in_specs=placed,
        out_specs=(P("probe", "blk"), P("probe", "blk"), P("probe", "blk")),
        check_vma=False,
    )
```

profile of v0, /device:TPU:8, one launch (start us, length us, event | category | flops | bytes accessed | tf_op | source)
XLA Modules:
  0.0 709.4 jit_solution(13328526686878321202)
XLA Ops:
  10.1 6.1 all-to-all-start
  16.3 58.9 %all-gather.2.cloned.1.call-done = bf16[2048,256]{1,0:T(8,128)(2,1)} async-done(((bf16[128,256]{1,0:T(8,128)(2,1)}), bf16[2048,256]{1,0:T(8,128)(2,1)}) %all-gather.2.cloned.1.call-update) | async-done | bytes 1048592 | tf_op jit(solution)/shard_map/all_gather | solution.py:26
  78.1 342.3 %while.14 = (s32[]{:T(128)}, bf16[128,256]{1,0:T(8,128)(2,1)S(1)}, bf16[64,128]{1,0:T(8,128)(2,1)S(1)}, f32[64,2048]{1,0:T(8,128)S(1)}, bf16[2048,256]{1,0:T(8,128)(2,1)S(1)}, /*index=5*/s32[]{:T(128)}) while((s32[]{:T(128)}, bf16[128,256]{1,0:T(8,128)(2,1)S(1)}, bf16[64,128]{1,0:T(8,128)(2,1)S(1)}, f32[64,2048]{1,0:T(8,128)S(1)}, ...), condition=%wide.region_7.0_spmd, body=%wide.region_4.7_spmd.sunk | while | flops 172717952 | bytes 3802261 | solution.py:42
  78.1 4.3 collective-permute-start
  89.3 3.4 collective-permute-start
  92.7 3.4 collective-permute-start.1
  99.7 4.3 collective-permute-start
  110.9 3.4 collective-permute-start
  114.3 3.5 collective-permute-start.1
  121.2 4.3 collective-permute-start
  132.5 3.8 collective-permute-start
  136.3 4.2 collective-permute-start.1
  143.4 4.9 collective-permute-start
  148.3 3.7 collective-permute-start.1
  155.3 4.6 collective-permute-start
  159.9 3.6 collective-permute-start.1
  166.8 4.5 collective-permute-start
  178.2 3.9 collective-permute-start
  189.0 4.1 collective-permute-start
  200.0 3.9 collective-permute-start
  210.9 4.1 collective-permute-start
  215.0 3.4 collective-permute-start.1
  222.0 4.4 collective-permute-start
  233.3 4.0 collective-permute-start
  237.2 3.7 collective-permute-start.1
  244.2 4.7 collective-permute-start
  255.8 3.9 collective-permute-start
  259.7 3.4 collective-permute-start.1
  266.6 4.3 collective-permute-start
  277.9 3.7 collective-permute-start
  288.5 4.0 collective-permute-start
  299.4 4.0 collective-permute-start
  303.5 3.3 collective-permute-start.1
  310.6 4.2 collective-permute-start
  321.7 4.1 collective-permute-start
  332.8 4.0 collective-permute-start
  343.7 4.1 collective-permute-start
  354.6 3.9 collective-permute-start
  358.5 3.4 collective-permute-start.1
  365.4 4.3 collective-permute-start
  376.6 3.8 collective-permute-start
  387.3 4.0 collective-permute-start
  398.3 4.0 collective-permute-start
  402.3 3.4 collective-permute-start.1
  409.2 4.3 collective-permute-start
  423.3 150.5 %all-reduce.4.cloned.1.call-done = f32[64,2048]{1,0:T(8,128)} async-done(((f32[64,2048]{1,0:T(8,128)}), f32[64,2048]{1,0:T(8,128)}) %all-reduce.4.cloned.1.call-update) | async-done | bytes 524304
  574.8 62.2 %all-reduce.1 = (f32[4]{0:T(128)S(1)}, f32[4]{0:T(128)S(1)}) all-reduce(f32[4]{0:T(128)S(1)} %multiply_reduce_fusion.6, f32[4]{0:T(128)S(1)} %multiply_reduce_fusion.5), channel_id=1, replica_groups=mesh['blk'=32,'probe'=16] {'blk'}, use_global_device_ids=true, to_apply=%region_1.0 | all-reduce | flops 8 | bytes 64 | tf_op jit(solution)/shard_map/psum | solution.py:48
  638.7 63.1 %psum.23 = f32[4]{0:T(128)S(1)} all-reduce(f32[4]{0:T(128)S(1)} %get-tuple-element.43), channel_id=1, replica_groups=mesh['blk'=32,'probe'=16] {'blk'}, use_global_device_ids=true, to_apply=%region_12.0 | all-reduce | flops 4 | bytes 32 | tf_op jit(solution)/shard_map/psum | solution.py:52
  (267 shorter events, 185.5 us)
Async XLA Ops:
  7.2 68.1 %all-gather.2.cloned.1.call-start = ((), (), s32[]{:S(2)}) async-start(), calls=%async_computation.1 | async-start | bytes 1114112 | tf_op jit(solution)/shard_map/all_gather | solution.py:26
  10.1 66.8 %all-to-all-start = ((bf16[4,16,128]{2,0,1:T(4,128)(2,1)}), bf16[4,16,128]{2,0,1:T(4,128)(2,1)S(1)}, u32[]{:S(2)}, u32[]{:S(2)}) async-start(bf16[4,16,128]{2,0,1:T(4,128)(2,1)} %convert_bitcast_fusion), calls=%async_computation | async-start | bytes 32768 | tf_op jit(solution)/shard_map/all_to_all | solution.py:28
  16.3 557.5 %all-reduce.4.cloned.1.call-start = ((), (), s32[]{:S(2)}) async-start(), calls=%async_computation.2 | async-start | bytes 1048576
  78.1 10.0 %collective-permute-start = (bf16[128,256]{1,0:T(8,128)(2,1)S(1)}, bf16[128,256]{1,0:T(8,128)(2,1)S(1)}, u32[]{:S(2)}, u32[]{:S(2)}) collective-permute-start(bf16[128,256]{1,0:T(8,128)(2,1)S(1)} %get-tuple-element.86), channel_id=1, source_target_pairs={{0,16},{16,32},{32,48},{48,64},{64,80},{80,96},{96,112},{112,128},... | collective-permute-start | bytes 196616 | tf_op jit(solution)/shard_map/while/body/eval_jaxpr/ppermute | solution.py:12
  82.4 5.6 collective-permute-start.1
  89.3 9.0 %collective-permute-start = (bf16[128,256]{1,0:T(8,128)(2,1)S(1)}, bf16[128,256]{1,0:T(8,128)(2,1)S(1)}, u32[]{:S(2)}, u32[]{:S(2)}) collective-permute-start(bf16[128,256]{1,0:T(8,128)(2,1)S(1)} %get-tuple-element.86), channel_id=1, source_target_pairs={{0,16},{16,32},{32,48},{48,64},{64,80},{80,96},{96,112},{112,128},... | collective-permute-start | bytes 196616 | tf_op jit(solution)/shard_map/while/body/eval_jaxpr/ppermute | solution.py:12
  92.7 5.6 collective-permute-start.1
  99.7 10.0 %collective-permute-start = (bf16[128,256]{1,0:T(8,128)(2,1)S(1)}, bf16[128,256]{1,0:T(8,128)(2,1)S(1)}, u32[]{:S(2)}, u32[]{:S(2)}) collective-permute-start(bf16[128,256]{1,0:T(8,128)(2,1)S(1)} %get-tuple-element.86), channel_id=1, source_target_pairs={{0,16},{16,32},{32,48},{48,64},{64,80},{80,96},{96,112},{112,128},... | collective-permute-start | bytes 196616 | tf_op jit(solution)/shard_map/while/body/eval_jaxpr/ppermute | solution.py:12
  104.0 5.6 collective-permute-start.1
  110.9 9.0 %collective-permute-start = (bf16[128,256]{1,0:T(8,128)(2,1)S(1)}, bf16[128,256]{1,0:T(8,128)(2,1)S(1)}, u32[]{:S(2)}, u32[]{:S(2)}) collective-permute-start(bf16[128,256]{1,0:T(8,128)(2,1)S(1)} %get-tuple-element.86), channel_id=1, source_target_pairs={{0,16},{16,32},{32,48},{48,64},{64,80},{80,96},{96,112},{112,128},... | collective-permute-start | bytes 196616 | tf_op jit(solution)/shard_map/while/body/eval_jaxpr/ppermute | solution.py:12
  121.2 10.0 %collective-permute-start = (bf16[128,256]{1,0:T(8,128)(2,1)S(1)}, bf16[128,256]{1,0:T(8,128)(2,1)S(1)}, u32[]{:S(2)}, u32[]{:S(2)}) collective-permute-start(bf16[128,256]{1,0:T(8,128)(2,1)S(1)} %get-tuple-element.86), channel_id=1, source_target_pairs={{0,16},{16,32},{32,48},{48,64},{64,80},{80,96},{96,112},{112,128},... | collective-permute-start | bytes 196616 | tf_op jit(solution)/shard_map/while/body/eval_jaxpr/ppermute | solution.py:12
  125.6 5.6 collective-permute-start.1
  132.5 9.6 %collective-permute-start = (bf16[128,256]{1,0:T(8,128)(2,1)S(1)}, bf16[128,256]{1,0:T(8,128)(2,1)S(1)}, u32[]{:S(2)}, u32[]{:S(2)}) collective-permute-start(bf16[128,256]{1,0:T(8,128)(2,1)S(1)} %get-tuple-element.86), channel_id=1, source_target_pairs={{0,16},{16,32},{32,48},{48,64},{64,80},{80,96},{96,112},{112,128},... | collective-permute-start | bytes 196616 | tf_op jit(solution)/shard_map/while/body/eval_jaxpr/ppermute | solution.py:12
  136.3 5.8 collective-permute-start.1
  143.4 10.6 %collective-permute-start = (bf16[128,256]{1,0:T(8,128)(2,1)S(1)}, bf16[128,256]{1,0:T(8,128)(2,1)S(1)}, u32[]{:S(2)}, u32[]{:S(2)}) collective-permute-start(bf16[128,256]{1,0:T(8,128)(2,1)S(1)} %get-tuple-element.86), channel_id=1, source_target_pairs={{0,16},{16,32},{32,48},{48,64},{64,80},{80,96},{96,112},{112,128},... | collective-permute-start | bytes 196616 | tf_op jit(solution)/shard_map/while/body/eval_jaxpr/ppermute | solution.py:12
  155.3 10.2 %collective-permute-start = (bf16[128,256]{1,0:T(8,128)(2,1)S(1)}, bf16[128,256]{1,0:T(8,128)(2,1)S(1)}, u32[]{:S(2)}, u32[]{:S(2)}) collective-permute-start(bf16[128,256]{1,0:T(8,128)(2,1)S(1)} %get-tuple-element.86), channel_id=1, source_target_pairs={{0,16},{16,32},{32,48},{48,64},{64,80},{80,96},{96,112},{112,128},... | collective-permute-start | bytes 196616 | tf_op jit(solution)/shard_map/while/body/eval_jaxpr/ppermute | solution.py:12
  166.8 10.2 %collective-permute-start = (bf16[128,256]{1,0:T(8,128)(2,1)S(1)}, bf16[128,256]{1,0:T(8,128)(2,1)S(1)}, u32[]{:S(2)}, u32[]{:S(2)}) collective-permute-start(bf16[128,256]{1,0:T(8,128)(2,1)S(1)} %get-tuple-element.86), channel_id=1, source_target_pairs={{0,16},{16,32},{32,48},{48,64},{64,80},{80,96},{96,112},{112,128},... | collective-permute-start | bytes 196616 | tf_op jit(solution)/shard_map/while/body/eval_jaxpr/ppermute | solution.py:12
  171.3 5.6 collective-permute-start.1
  178.2 9.5 %collective-permute-start = (bf16[128,256]{1,0:T(8,128)(2,1)S(1)}, bf16[128,256]{1,0:T(8,128)(2,1)S(1)}, u32[]{:S(2)}, u32[]{:S(2)}) collective-permute-start(bf16[128,256]{1,0:T(8,128)(2,1)S(1)} %get-tuple-element.86), channel_id=1, source_target_pairs={{0,16},{16,32},{32,48},{48,64},{64,80},{80,96},{96,112},{112,128},... | collective-permute-start | bytes 196616 | tf_op jit(solution)/shard_map/while/body/eval_jaxpr/ppermute | solution.py:12
  182.1 5.6 collective-permute-start.1
  189.0 9.8 %collective-permute-start = (bf16[128,256]{1,0:T(8,128)(2,1)S(1)}, bf16[128,256]{1,0:T(8,128)(2,1)S(1)}, u32[]{:S(2)}, u32[]{:S(2)}) collective-permute-start(bf16[128,256]{1,0:T(8,128)(2,1)S(1)} %get-tuple-element.86), channel_id=1, source_target_pairs={{0,16},{16,32},{32,48},{48,64},{64,80},{80,96},{96,112},{112,128},... | collective-permute-start | bytes 196616 | tf_op jit(solution)/shard_map/while/body/eval_jaxpr/ppermute | solution.py:12
  193.1 5.6 collective-permute-start.1
  200.0 9.6 %collective-permute-start = (bf16[128,256]{1,0:T(8,128)(2,1)S(1)}, bf16[128,256]{1,0:T(8,128)(2,1)S(1)}, u32[]{:S(2)}, u32[]{:S(2)}) collective-permute-start(bf16[128,256]{1,0:T(8,128)(2,1)S(1)} %get-tuple-element.86), channel_id=1, source_target_pairs={{0,16},{16,32},{32,48},{48,64},{64,80},{80,96},{96,112},{112,128},... | collective-permute-start | bytes 196616 | tf_op jit(solution)/shard_map/while/body/eval_jaxpr/ppermute | solution.py:12
  204.0 5.6 collective-permute-start.1
  210.9 9.8 %collective-permute-start = (bf16[128,256]{1,0:T(8,128)(2,1)S(1)}, bf16[128,256]{1,0:T(8,128)(2,1)S(1)}, u32[]{:S(2)}, u32[]{:S(2)}) collective-permute-start(bf16[128,256]{1,0:T(8,128)(2,1)S(1)} %get-tuple-element.86), channel_id=1, source_target_pairs={{0,16},{16,32},{32,48},{48,64},{64,80},{80,96},{96,112},{112,128},... | collective-permute-start | bytes 196616 | tf_op jit(solution)/shard_map/while/body/eval_jaxpr/ppermute | solution.py:12
  215.0 5.7 collective-permute-start.1
  222.0 10.0 %collective-permute-start = (bf16[128,256]{1,0:T(8,128)(2,1)S(1)}, bf16[128,256]{1,0:T(8,128)(2,1)S(1)}, u32[]{:S(2)}, u32[]{:S(2)}) collective-permute-start(bf16[128,256]{1,0:T(8,128)(2,1)S(1)} %get-tuple-element.86), channel_id=1, source_target_pairs={{0,16},{16,32},{32,48},{48,64},{64,80},{80,96},{96,112},{112,128},... | collective-permute-start | bytes 196616 | tf_op jit(solution)/shard_map/while/body/eval_jaxpr/ppermute | solution.py:12
  233.3 9.6 %collective-permute-start = (bf16[128,256]{1,0:T(8,128)(2,1)S(1)}, bf16[128,256]{1,0:T(8,128)(2,1)S(1)}, u32[]{:S(2)}, u32[]{:S(2)}) collective-permute-start(bf16[128,256]{1,0:T(8,128)(2,1)S(1)} %get-tuple-element.86), channel_id=1, source_target_pairs={{0,16},{16,32},{32,48},{48,64},{64,80},{80,96},{96,112},{112,128},... | collective-permute-start | bytes 196616 | tf_op jit(solution)/shard_map/while/body/eval_jaxpr/ppermute | solution.py:12
  237.2 5.7 collective-permute-start.1
  244.2 10.3 %collective-permute-start = (bf16[128,256]{1,0:T(8,128)(2,1)S(1)}, bf16[128,256]{1,0:T(8,128)(2,1)S(1)}, u32[]{:S(2)}, u32[]{:S(2)}) collective-permute-start(bf16[128,256]{1,0:T(8,128)(2,1)S(1)} %get-tuple-element.86), channel_id=1, source_target_pairs={{0,16},{16,32},{32,48},{48,64},{64,80},{80,96},{96,112},{112,128},... | collective-permute-start | bytes 196616 | tf_op jit(solution)/shard_map/while/body/eval_jaxpr/ppermute | solution.py:12
  248.9 5.6 collective-permute-start.1
  255.8 9.6 %collective-permute-start = (bf16[128,256]{1,0:T(8,128)(2,1)S(1)}, bf16[128,256]{1,0:T(8,128)(2,1)S(1)}, u32[]{:S(2)}, u32[]{:S(2)}) collective-permute-start(bf16[128,256]{1,0:T(8,128)(2,1)S(1)} %get-tuple-element.86), channel_id=1, source_target_pairs={{0,16},{16,32},{32,48},{48,64},{64,80},{80,96},{96,112},{112,128},... | collective-permute-start | bytes 196616 | tf_op jit(solution)/shard_map/while/body/eval_jaxpr/ppermute | solution.py:12
  266.6 10.0 %collective-permute-start = (bf16[128,256]{1,0:T(8,128)(2,1)S(1)}, bf16[128,256]{1,0:T(8,128)(2,1)S(1)}, u32[]{:S(2)}, u32[]{:S(2)}) collective-permute-start(bf16[128,256]{1,0:T(8,128)(2,1)S(1)} %get-tuple-element.86), channel_id=1, source_target_pairs={{0,16},{16,32},{32,48},{48,64},{64,80},{80,96},{96,112},{112,128},... | collective-permute-start | bytes 196616 | tf_op jit(solution)/shard_map/while/body/eval_jaxpr/ppermute | solution.py:12
  277.9 9.3 %collective-permute-start = (bf16[128,256]{1,0:T(8,128)(2,1)S(1)}, bf16[128,256]{1,0:T(8,128)(2,1)S(1)}, u32[]{:S(2)}, u32[]{:S(2)}) collective-permute-start(bf16[128,256]{1,0:T(8,128)(2,1)S(1)} %get-tuple-element.86), channel_id=1, source_target_pairs={{0,16},{16,32},{32,48},{48,64},{64,80},{80,96},{96,112},{112,128},... | collective-permute-start | bytes 196616 | tf_op jit(solution)/shard_map/while/body/eval_jaxpr/ppermute | solution.py:12
  288.5 9.7 %collective-permute-start = (bf16[128,256]{1,0:T(8,128)(2,1)S(1)}, bf16[128,256]{1,0:T(8,128)(2,1)S(1)}, u32[]{:S(2)}, u32[]{:S(2)}) collective-permute-start(bf16[128,256]{1,0:T(8,128)(2,1)S(1)} %get-tuple-element.86), channel_id=1, source_target_pairs={{0,16},{16,32},{32,48},{48,64},{64,80},{80,96},{96,112},{112,128},... | collective-permute-start | bytes 196616 | tf_op jit(solution)/shard_map/while/body/eval_jaxpr/ppermute | solution.py:12
  299.4 9.8 %collective-permute-start = (bf16[128,256]{1,0:T(8,128)(2,1)S(1)}, bf16[128,256]{1,0:T(8,128)(2,1)S(1)}, u32[]{:S(2)}, u32[]{:S(2)}) collective-permute-start(bf16[128,256]{1,0:T(8,128)(2,1)S(1)} %get-tuple-element.86), channel_id=1, source_target_pairs={{0,16},{16,32},{32,48},{48,64},{64,80},{80,96},{96,112},{112,128},... | collective-permute-start | bytes 196616 | tf_op jit(solution)/shard_map/while/body/eval_jaxpr/ppermute | solution.py:12
  303.5 5.8 collective-permute-start.1
  310.6 9.9 %collective-permute-start = (bf16[128,256]{1,0:T(8,128)(2,1)S(1)}, bf16[128,256]{1,0:T(8,128)(2,1)S(1)}, u32[]{:S(2)}, u32[]{:S(2)}) collective-permute-start(bf16[128,256]{1,0:T(8,128)(2,1)S(1)} %get-tuple-element.86), channel_id=1, source_target_pairs={{0,16},{16,32},{32,48},{48,64},{64,80},{80,96},{96,112},{112,128},... | collective-permute-start | bytes 196616 | tf_op jit(solution)/shard_map/while/body/eval_jaxpr/ppermute | solution.py:12
  321.7 9.8 %collective-permute-start = (bf16[128,256]{1,0:T(8,128)(2,1)S(1)}, bf16[128,256]{1,0:T(8,128)(2,1)S(1)}, u32[]{:S(2)}, u32[]{:S(2)}) collective-permute-start(bf16[128,256]{1,0:T(8,128)(2,1)S(1)} %get-tuple-element.86), channel_id=1, source_target_pairs={{0,16},{16,32},{32,48},{48,64},{64,80},{80,96},{96,112},{112,128},... | collective-permute-start | bytes 196616 | tf_op jit(solution)/shard_map/while/body/eval_jaxpr/ppermute | solution.py:12
  325.8 5.7 collective-permute-start.1
  332.8 9.6 %collective-permute-start = (bf16[128,256]{1,0:T(8,128)(2,1)S(1)}, bf16[128,256]{1,0:T(8,128)(2,1)S(1)}, u32[]{:S(2)}, u32[]{:S(2)}) collective-permute-start(bf16[128,256]{1,0:T(8,128)(2,1)S(1)} %get-tuple-element.86), channel_id=1, source_target_pairs={{0,16},{16,32},{32,48},{48,64},{64,80},{80,96},{96,112},{112,128},... | collective-permute-start | bytes 196616 | tf_op jit(solution)/shard_map/while/body/eval_jaxpr/ppermute | solution.py:12
  343.7 9.7 %collective-permute-start = (bf16[128,256]{1,0:T(8,128)(2,1)S(1)}, bf16[128,256]{1,0:T(8,128)(2,1)S(1)}, u32[]{:S(2)}, u32[]{:S(2)}) collective-permute-start(bf16[128,256]{1,0:T(8,128)(2,1)S(1)} %get-tuple-element.86), channel_id=1, source_target_pairs={{0,16},{16,32},{32,48},{48,64},{64,80},{80,96},{96,112},{112,128},... | collective-permute-start | bytes 196616 | tf_op jit(solution)/shard_map/while/body/eval_jaxpr/ppermute | solution.py:12
  354.6 9.5 %collective-permute-start = (bf16[128,256]{1,0:T(8,128)(2,1)S(1)}, bf16[128,256]{1,0:T(8,128)(2,1)S(1)}, u32[]{:S(2)}, u32[]{:S(2)}) collective-permute-start(bf16[128,256]{1,0:T(8,128)(2,1)S(1)} %get-tuple-element.86), channel_id=1, source_target_pairs={{0,16},{16,32},{32,48},{48,64},{64,80},{80,96},{96,112},{112,128},... | collective-permute-start | bytes 196616 | tf_op jit(solution)/shard_map/while/body/eval_jaxpr/ppermute | solution.py:12
  365.4 9.9 %collective-permute-start = (bf16[128,256]{1,0:T(8,128)(2,1)S(1)}, bf16[128,256]{1,0:T(8,128)(2,1)S(1)}, u32[]{:S(2)}, u32[]{:S(2)}) collective-permute-start(bf16[128,256]{1,0:T(8,128)(2,1)S(1)} %get-tuple-element.86), channel_id=1, source_target_pairs={{0,16},{16,32},{32,48},{48,64},{64,80},{80,96},{96,112},{112,128},... | collective-permute-start | bytes 196616 | tf_op jit(solution)/shard_map/while/body/eval_jaxpr/ppermute | solution.py:12
  376.6 9.4 %collective-permute-start = (bf16[128,256]{1,0:T(8,128)(2,1)S(1)}, bf16[128,256]{1,0:T(8,128)(2,1)S(1)}, u32[]{:S(2)}, u32[]{:S(2)}) collective-permute-start(bf16[128,256]{1,0:T(8,128)(2,1)S(1)} %get-tuple-element.86), channel_id=1, source_target_pairs={{0,16},{16,32},{32,48},{48,64},{64,80},{80,96},{96,112},{112,128},... | collective-permute-start | bytes 196616 | tf_op jit(solution)/shard_map/while/body/eval_jaxpr/ppermute | solution.py:12
  387.3 9.7 %collective-permute-start = (bf16[128,256]{1,0:T(8,128)(2,1)S(1)}, bf16[128,256]{1,0:T(8,128)(2,1)S(1)}, u32[]{:S(2)}, u32[]{:S(2)}) collective-permute-start(bf16[128,256]{1,0:T(8,128)(2,1)S(1)} %get-tuple-element.86), channel_id=1, source_target_pairs={{0,16},{16,32},{32,48},{48,64},{64,80},{80,96},{96,112},{112,128},... | collective-permute-start | bytes 196616 | tf_op jit(solution)/shard_map/while/body/eval_jaxpr/ppermute | solution.py:12
  398.3 9.7 %collective-permute-start = (bf16[128,256]{1,0:T(8,128)(2,1)S(1)}, bf16[128,256]{1,0:T(8,128)(2,1)S(1)}, u32[]{:S(2)}, u32[]{:S(2)}) collective-permute-start(bf16[128,256]{1,0:T(8,128)(2,1)S(1)} %get-tuple-element.86), channel_id=1, source_target_pairs={{0,16},{16,32},{32,48},{48,64},{64,80},{80,96},{96,112},{112,128},... | collective-permute-start | bytes 196616 | tf_op jit(solution)/shard_map/while/body/eval_jaxpr/ppermute | solution.py:12
  409.2 9.9 %collective-permute-start = (bf16[128,256]{1,0:T(8,128)(2,1)S(1)}, bf16[128,256]{1,0:T(8,128)(2,1)S(1)}, u32[]{:S(2)}, u32[]{:S(2)}) collective-permute-start(bf16[128,256]{1,0:T(8,128)(2,1)S(1)} %get-tuple-element.86), channel_id=1, source_target_pairs={{0,16},{16,32},{32,48},{48,64},{64,80},{80,96},{96,112},{112,128},... | collective-permute-start | bytes 196616 | tf_op jit(solution)/shard_map/while/body/eval_jaxpr/ppermute | solution.py:12
  (24 other events, 1630.2 us)
Sparse Core Ops, SparseCore 0:
  11.3 63.8 all-gather.1
  421.4 152.3 all-reduce.3
where the time goes:
time: 712 us; the launch traced here: 709 us
  waiting for transfers between devices  274 us (38%)
  starting transfers between devices  233 us (33%)
  blocking collectives  125 us (18%)
  matrix products  36 us (5%)
  other arithmetic  21.9 us (3%)
  between operations  14.8 us (2%)
    ppermute x62, starting transfers between devices, shifted(): lax.ppermute(shard, axis, [(i, (i + by) % devices) for i in range(devices)])  227 us
    unnamed x3, waiting for transfers between devices  150 us
    ppermute x62, waiting for transfers between devices, shifted(): lax.ppermute(shard, axis, [(i, (i + by) % devices) for i in range(devices)])  64.8 us
    psum x1, blocking collectives, shards(): new_norm = lax.psum(jnp.sum(new_residual * new_residual, axis=1), 'blk')  63.1 us
    psum x1, blocking collectives, shards(): old_norm = lax.psum(jnp.sum(residual * residual, axis=1), 'blk')  62.2 us
    all_gather x1, waiting for transfers between devices, shards(): block_pts = lax.all_gather(own_rows, 'probe', axis=0, tiled=True)  58.9 us
    dot_general x31, matrix products, advance(): jnp.dot(moving_dir, kernel_tile(moving_pts, block_pts), preferred_element...  34.9 us
  transfers between devices with their start and end apart: 65, of which 33 were waited for; matrix products, arithmetic and copies ran while one was open for 2% of the time, Pallas kernels for 0%

commit v1 on v0

v1 whole, which is shorter than its diff:
```python
import functools
import math

import jax
import jax.numpy as jnp
from jax import lax
from jax.experimental import pallas as pl
from jax.experimental.pallas import tpu as pltpu
from jax.sharding import Mesh, PartitionSpec as P

noise_var = 0.1
epsilon = 1e-06

LOG2E = 1.0 / math.log(2.0)
EXPONENT = -math.sqrt(5.0) * LOG2E
LINEAR = -3.0 * LOG2E
CONSTANT = 3.0 * LOG2E * LOG2E
LEADING = 1.0 / CONSTANT

BLOCK = ("z", "ylo")
PROBE = ("yhi", "x", "core")
PLANE = ("ylo", "yhi", "x", "core")
CHIPS = ("ylo", "yhi", "x")

FEAT = 256
PROBES = 64
OWN_POINTS = 128
OWN_PROBES = 4
PACKED = OWN_POINTS + PROBES * OWN_POINTS // FEAT
COLS = 512
TOGETHER = 2
ROWS = 256
SLICE = 32


def prepare(row_refs, points, norms, dirs):
    at = 0
    for ref in row_refs:
        for chunk in range(ref.shape[0]):
            here = slice(at, at + OWN_POINTS)
            rows = jnp.transpose(ref[chunk, :OWN_POINTS, :].astype(jnp.float32))
            points[:, here] = (rows * -2.0).astype(jnp.bfloat16)
            norms[:, here] = jnp.broadcast_to(
                jnp.sum(rows * rows, axis=0, keepdims=True), (8, OWN_POINTS)
            )
            low = ref[chunk, OWN_POINTS:, :].astype(jnp.float32)
            low = jnp.concatenate(
                [low[:, :OWN_POINTS], low[:, OWN_POINTS:], jnp.zeros((PROBES, OWN_POINTS))]
            )
            dirs[here, :] = jnp.transpose(low).astype(jnp.bfloat16)
            at += OWN_POINTS


def first_kernel(n_sources, *refs):
    row_refs, refs = refs[:n_sources], refs[n_sources:]
    cols, out_ref, col_norms, *scratch = refs

    @pl.loop(0, cols.shape[0] // COLS)
    def _(at):
        here = pl.ds(pl.multiple_of(at * COLS, COLS), COLS)
        wide = cols[here, :].astype(jnp.float32)
        col_norms[here, :] = jnp.broadcast_to(
            jnp.sum(wide * wide, axis=1, keepdims=True), (COLS, 128)
        )

    tiles(row_refs, cols, col_norms, None, out_ref, *scratch)


def next_kernel(n_sources, *refs):
    row_refs, refs = refs[:n_sources], refs[n_sources:]
    cols, col_norms, carry_ref, out_ref, *scratch = refs
    tiles(row_refs, cols, col_norms, carry_ref, out_ref, *scratch)


def tiles(
    row_refs, cols, col_norms, carry_ref, out_ref, points, norms, dirs, inners, values
):
    prepare(row_refs, points, norms, dirs)
    n_rows, n_cols = points.shape[1], cols.shape[0]
    tops = [(top, min(ROWS, n_rows - top)) for top in range(0, n_rows, ROWS)]
    steps = [(left, top, rows) for left in range(TOGETHER) for top, rows in tops]

    def block(at):
        return pl.ds(pl.multiple_of(at * COLS, COLS), COLS)

    def inner(slot, top, rows, here):
        inners[slot, :, :rows] = jnp.dot(
            cols[here, :], points[:, top : top + rows], preferred_element_type=jnp.float32
        )

    def kernel_values(slot, top, rows, at):
        for col in range(0, COLS, SLICE):
            there = pl.ds(pl.multiple_of(at * COLS, COLS) + col, SLICE)
            own_norms = col_norms[there, :]
            for row in range(0, rows, 128):
                squared = inners[slot, col : col + SLICE, row : row + 128] + own_norms
                squared = squared.reshape(SLICE // 8, 8, 128)
                squared = squared + norms[:, top + row : top + row + 128]
                squared = jnp.maximum(squared, 1e-30)
                power = squared * lax.rsqrt(squared) * EXPONENT
                value = ((power + LINEAR) * power + CONSTANT) * jnp.exp2(power)
                values[slot, col : col + SLICE, row : row + 128] = value.reshape(
                    SLICE, 128
                ).astype(jnp.bfloat16)

    def weighted(slot, top, rows):
        return jnp.dot(
            values[slot, :, :rows], dirs[top : top + rows, :], preferred_element_type=jnp.float32
        )

    def finish(at, total):
        if len(out_ref.shape) == 2:
            out_ref[block(at), :] = total
        else:
            width = out_ref.shape[2] // COLS
            groups = PROBES // OWN_PROBES
            total = jnp.transpose(total)[:PROBES] * LEADING
            out_ref[pl.ds(at // width * groups, groups), :, block(at % width)] = total.astype(
                jnp.bfloat16
            ).reshape(groups, OWN_PROBES, COLS)

    last_block = n_cols // COLS - 1
    inner(0, *tops[0], block(0))

    @pl.loop(0, n_cols // (COLS * TOGETHER))
    def _(turn):
        first = turn * TOGETHER

        def add(step, total):
            left, top, rows = steps[step]
            part = weighted(step % 2, top, rows)
            if top:
                part = total + part
            elif carry_ref is not None:
                part = part + carry_ref[block(first + left), :]
            if top + rows == n_rows:
                finish(first + left, part)
            return part

        total = None
        for step, (left, top, rows) in enumerate(steps):
            if step + 1 < len(steps):
                next_left, next_top, next_rows = steps[step + 1]
                inner((step + 1) % 2, next_top, next_rows, block(first + next_left))
            else:
                inner(0, *tops[0], block(jnp.minimum(first + TOGETHER, last_block)))
            kernel_values(step % 2, top, rows, first + left)
            if step:
                total = add(step - 1, total)
        add(len(steps) - 1, total)


WHOLE = pl.BlockSpec(memory_space=pltpu.VMEM)


def product_call(kernel, sources, others, n_cols, out_shape):
    n_rows = sum(source.shape[0] for source in sources) * OWN_POINTS
    return pl.pallas_call(
        functools.partial(kernel, len(sources)),
        in_specs=[WHOLE] * (len(sources) + len(others)),
        out_specs=jax.tree.map(lambda _: WHOLE, out_shape),
        out_shape=out_shape,
        scratch_shapes=[
            pltpu.VMEM((FEAT, n_rows), jnp.bfloat16),
            pltpu.VMEM((8, n_rows), jnp.float32),
            pltpu.VMEM((n_rows, 128), jnp.bfloat16),
            pltpu.VMEM((2, COLS, ROWS), jnp.float32),
            pltpu.VMEM((2, COLS, ROWS), jnp.bfloat16),
        ],
        compiler_params=pltpu.CompilerParams(vmem_limit_bytes=32 * 1024 * 1024),
    )(*sources, *others)


def first_product(sources, cols):
    whole = jax.ShapeDtypeStruct((cols.shape[0], 128), jnp.float32)
    return product_call(first_kernel, sources, [cols], cols.shape[0], [whole, whole])


def tile_product(sources, cols, col_norms, carry, last=False):
    n_cols = cols.shape[0]
    halves = 2
    if last:
        out_shape = jax.ShapeDtypeStruct(
            (halves * PROBES // OWN_PROBES, OWN_PROBES, n_cols // halves), jnp.bfloat16
        )
    else:
        out_shape = jax.ShapeDtypeStruct((n_cols, 128), jnp.float32)
    return product_call(next_kernel, sources, [cols, col_norms, carry], n_cols, out_shape)


def to_all(own, axes):
    return lax.all_to_all(
        jnp.broadcast_to(own[None], (lax.axis_size(axes),) + own.shape),
        axes,
        split_axis=0,
        concat_axis=0,
        tiled=True,
    )


def from_z(shard, by, core_by=None):
    devices = lax.axis_size("z")
    steps = (by, by if core_by is None else core_by)
    pairs = [
        (2 * ((z + steps[core]) % devices) + core, 2 * z + core)
        for z in range(devices)
        for core in range(2)
    ]
    return lax.ppermute(shard, ("z", "core"), pairs)


def shards(points, inv_length, solution, residual, direction):
    own_rows = (points.astype(jnp.float32) * inv_length[None, :]).astype(jnp.bfloat16)
    low_direction = direction.astype(jnp.bfloat16)
    own_dirs = lax.all_to_all(low_direction, PROBE, split_axis=1, concat_axis=0, tiled=True)
    plane_rows, own_dirs = lax.optimization_barrier((own_rows, own_dirs))
    half = PROBES // 2
    packed = jnp.concatenate(
        [own_rows, jnp.concatenate([own_dirs[:half], own_dirs[half:]], axis=1)], axis=0
    )
    first_core = lax.axis_index("core") == 0

    own_half = to_all(plane_rows, CHIPS)

    ahead = from_z(packed, 4)
    behind = from_z(packed, -4)
    own_half, ahead, behind = lax.optimization_barrier((own_half, ahead, behind))
    far = jnp.stack([packed, ahead, behind])
    above = from_z(far, 1)
    below = from_z(far, -1)
    opposite = from_z(jnp.where(first_core, ahead, behind), 4, -4)
    other_half = lax.ppermute(own_half, "core", [(0, 1), (1, 0)])
    cols = jnp.where(
        first_core,
        jnp.stack([own_half, other_half], axis=1),
        jnp.stack([other_half, own_half], axis=1),
    ).reshape(-1, FEAT)
    partial_value, col_norms = first_product([far], cols)

    far, opposite, above, below, partial_value = lax.optimization_barrier(
        (far, opposite[None], above, below, partial_value)
    )
    second = from_z(jnp.concatenate([far, opposite]), 2, -2)
    last_above = from_z(opposite, 1)
    last_below = from_z(opposite, -1)
    partial_value = tile_product([above, below], cols, col_norms, partial_value)
    partial_value = tile_product(
        [opposite, second, last_above, last_below], cols, col_norms, partial_value, last=True
    )
    pieces = lax.all_to_all(partial_value, PLANE, split_axis=0, concat_axis=0, tiled=True)
    image = jnp.sum(pieces.astype(jnp.float32), axis=0) + noise_var * low_direction.astype(
        jnp.float32
    )
    sums = jnp.stack(
        [
            jnp.sum(residual * residual, axis=1),
            jnp.sum(direction * image, axis=1),
            jnp.sum(residual * image, axis=1),
            jnp.sum(image * image, axis=1),
        ]
    )
    sums = jnp.sum(to_all(sums, BLOCK), axis=0)
    old_norm, curvature, cross, image_norm = sums[0], sums[1], sums[2], sums[3]
    step_len = old_norm / curvature
    new_norm = jnp.maximum(old_norm - step_len * (2.0 * cross - step_len * image_norm), 0.0)
    new_solution = solution + step_len[:, None] * direction
    new_residual = residual - step_len[:, None] * image
    new_direction = new_residual + (new_norm / (old_norm + epsilon))[:, None] * direction
    return (new_solution, new_residual, new_direction)


def solution(mesh):
    fine = Mesh(
        mesh.devices.reshape(16, 2, 2, 4, 2), ("z", "ylo", "yhi", "x", "core")
    )
    placed = (P(BLOCK + PROBE, None), P(), P(PROBE, BLOCK), P(PROBE, BLOCK), P(PROBE, BLOCK))
    return jax.shard_map(
        shards,
        mesh=fine,
        in_specs=placed,
        out_specs=(P(PROBE, BLOCK), P(PROBE, BLOCK), P(PROBE, BLOCK)),
        check_vma=False,
    )
```

time: 712 us -> 137 us (0.19)
  waiting for transfers between devices: 274 us -> 19.2 us
  starting transfers between devices: 233 us -> 49.9 us
  blocking collectives: 125 us -> 39 us
  matrix products: 36 us -> 0 us
  Pallas kernels: 0 us -> 22.3 us
  other arithmetic: 21.9 us -> 3.69 us
  between operations: 14.8 us -> 0.87 us
    ppermute x62 -> x9, starting transfers between devices: 227 us -> 37.2 us  [the longest x8 35.3 us: from_z(): return lax.ppermute(shard, ('z', 'core'), pairs)]
    unnamed x3 -> x0, waiting for transfers between devices: 150 us -> none
    psum x2 -> x0, blocking collectives: 125 us -> none  [the longest x1 63.1 us: shards(): new_norm = lax.psum(jnp.sum(new_residual * new_residual, axis=1), 'blk')]
    all_gather x1 -> x0, waiting for transfers between devices: 58.9 us -> none  [shards(): block_pts = lax.all_gather(own_rows, 'probe', axis=0, tiled=True)]
    ppermute x62 -> x9, waiting for transfers between devices: 64.8 us -> 12.5 us  [the longest x8 12.5 us: from_z(): return lax.ppermute(shard, ('z', 'core'), pairs)]
    all_to_all x0 -> x2, blocking collectives: none -> 39 us  [the longest x1 21.7 us: to_all(): lax.all_to_all(jnp.broadcast_to(own[None], (lax.axis_size(axes),) + own.s...]
    dot_general x32 -> x0, matrix products: 36 us -> none  [the longest x31 34.9 us: advance(): jnp.dot(moving_dir, kernel_tile(moving_pts, block_pts), preferred_element...]
    pallas_call x0 -> x3, Pallas kernels: none -> 22.3 us  [product_call(): pl.pallas_call(functools.partial(kernel, len(sources)), in_specs=[WHOLE]...]
  transfers between devices with their start and end apart: 65 -> 11, of which waited for: 33 -> 5; matrix products, arithmetic and copies ran while one was open for 2% -> 1% of each run, Pallas kernels for 0% -> 10%
where the time goes in v1:
time: 137 us; the launch traced here: 136 us
  starting transfers between devices  49.9 us (36%)
  blocking collectives  39 us (28%)
  Pallas kernels  22.3 us (16%)
  waiting for transfers between devices  19.2 us (14%)
  other arithmetic  3.69 us (3%)
    ppermute x8, starting transfers between devices, from_z(): return lax.ppermute(shard, ('z', 'core'), pairs)  35.3 us
    pallas_call x3, Pallas kernels, product_call(): pl.pallas_call(functools.partial(kernel, len(sources)), in_specs=[WHOLE]...  22.3 us
    all_to_all x1, blocking collectives, to_all(): lax.all_to_all(jnp.broadcast_to(own[None], (lax.axis_size(axes),) + own.s...  21.7 us
    all_to_all x1, blocking collectives, shards(): lax.all_to_all(partial_value, PLANE, split_axis=0, concat_axis=0, tiled=T...  17.3 us
    ppermute x8, waiting for transfers between devices, from_z(): return lax.ppermute(shard, ('z', 'core'), pairs)  12.5 us
    all_to_all x1, waiting for transfers between devices, shards(): lax.all_to_all(low_direction, PROBE, split_axis=1, concat_axis=0, tiled=T...  6.72 us
    all_to_all x1, starting transfers between devices, to_all(): lax.all_to_all(jnp.broadcast_to(own[None], (lax.axis_size(axes),) + own.s...  6.62 us
    all_to_all x1, starting transfers between devices, shards(): lax.all_to_all(low_direction, PROBE, split_axis=1, concat_axis=0, tiled=T...  6.14 us
  transfers between devices with their start and end apart: 11, of which 5 were waited for; matrix products, arithmetic and copies ran while one was open for 1% of the time, Pallas kernels for 10%

profile of v1, /device:TPU:8, one launch (start us, length us, event | category | flops | bytes accessed | tf_op | source)
XLA Modules:
  0.0 136.1 jit_solution(11917893637776431292)
XLA Ops:
  0.6 1.4 %convert_bitcast_fusion = bf16[4,16,128]{2,0,1:T(4,128)(2,1)} fusion(f32[4,2048]{1,0:T(4,128)} %param.9), kind=kLoop, calls=%fused_computation.15 | loop fusion | flops 8192 | bytes 49152 | tf_op jit(solution)/shard_map/all_to_all | solution.py:215
  2.0 6.1 %all-to-all-start = ((bf16[4,16,128]{2,0,1:T(4,128)(2,1)}), bf16[4,16,128]{2,0,1:T(4,128)(2,1)S(1)}, u32[]{:S(2)}, u32[]{:S(2)}) async-start(bf16[4,16,128]{2,0,1:T(4,128)(2,1)} %convert_bitcast_fusion), calls=%async_computation | async-start | bytes 32768 | tf_op jit(solution)/shard_map/all_to_all | solution.py:215
  8.1 0.9 multiply_convert_fusion
  9.0 6.7 %all-to-all-done = bf16[4,16,128]{2,0,1:T(4,128)(2,1)S(1)} async-done(((bf16[4,16,128]{2,0,1:T(4,128)(2,1)}), bf16[4,16,128]{2,0,1:T(4,128)(2,1)S(1)}, u32[]{:S(2)}, u32[]{:S(2)}) %all-to-all-start) | async-done | bytes 16416 | tf_op jit(solution)/shard_map/all_to_all | solution.py:215
  15.7 1.1 broadcast_in_dim.6
  16.8 6.6 %all-to-all-start.1 = ((bf16[16,128,256]{2,1,0:T(8,128)(2,1)}), bf16[16,128,256]{2,1,0:T(8,128)(2,1)S(1)}, u32[]{:S(2)}, u32[]{:S(2)}) async-start(bf16[16,128,256]{2,1,0:T(8,128)(2,1)} %broadcast_in_dim.6), calls=%async_computation.1 | async-start | bytes 2097152 | tf_op jit(solution)/shard_map/all_to_all | solution.py:192
  23.4 11.0 %collective-permute-start = (bf16[160,256]{1,0:T(8,128)(2,1)S(1)}, bf16[160,256]{1,0:T(8,128)(2,1)S(1)}, u32[]{:S(2)}, u32[]{:S(2)}) collective-permute-start(bf16[160,256]{1,0:T(8,128)(2,1)S(1)} %get-tuple-element.36), channel_id=1, source_target_pairs={{128,0},{129,1},{160,32},{161,33},{192,64},{193,65},{224,96},{225,... | collective-permute-start | bytes 245768 | tf_op jit(solution)/shard_map/ppermute | solution.py:209
  34.4 1.9 %collective-permute-start.1 = (bf16[160,256]{1,0:T(8,128)(2,1)S(1)}, bf16[160,256]{1,0:T(8,128)(2,1)S(1)}, u32[]{:S(2)}, u32[]{:S(2)}) collective-permute-start(bf16[160,256]{1,0:T(8,128)(2,1)S(1)} %get-tuple-element.36), channel_id=1, source_target_pairs={{384,0},{385,1},{416,32},{417,33},{448,64},{449,65},{480,96},{481,... | collective-permute-start | bytes 245768 | tf_op jit(solution)/shard_map/ppermute | solution.py:209
  36.3 5.1 %collective-permute-done = bf16[160,256]{1,0:T(8,128)(2,1)S(1)} collective-permute-done((bf16[160,256]{1,0:T(8,128)(2,1)S(1)}, bf16[160,256]{1,0:T(8,128)(2,1)S(1)}, u32[]{:S(2)}, u32[]{:S(2)}) %collective-permute-start) | collective-permute-done | bytes 81952 | tf_op jit(solution)/shard_map/ppermute | solution.py:209
  41.4 5.0 %collective-permute-done.1 = bf16[160,256]{1,0:T(8,128)(2,1)S(1)} collective-permute-done((bf16[160,256]{1,0:T(8,128)(2,1)S(1)}, bf16[160,256]{1,0:T(8,128)(2,1)S(1)}, u32[]{:S(2)}, u32[]{:S(2)}) %collective-permute-start.1) | collective-permute-done | bytes 81952 | tf_op jit(solution)/shard_map/ppermute | solution.py:209
  46.4 0.0 all-to-all-done.1
  46.4 1.9 %collective-permute-start.5 = (bf16[16,128,256]{2,1,0:T(8,128)(2,1)S(1)}, bf16[16,128,256]{2,1,0:T(8,128)(2,1)S(1)}, u32[]{:S(2)}, u32[]{:S(2)}) collective-permute-start(bf16[16,128,256]{2,1,0:T(8,128)(2,1)S(1)} %all-to-all-done.1), channel_id=1, source_target_pairs={{0,1},{1,0},{2,3},{3,2},{4,5},{5,4},{6,7},{7,6},{8,9},{9,8},{10,11... | collective-permute-start | bytes 3145736 | tf_op jit(solution)/shard_map/ppermute | solution.py:232
  48.3 7.1 %collective-permute-start.3 = (bf16[3,160,256]{2,1,0:T(8,128)(2,1)S(1)}, bf16[3,160,256]{2,1,0:T(8,128)(2,1)S(1)}, u32[]{:S(2)}, u32[]{:S(2)}) collective-permute-start(bf16[3,160,256]{2,1,0:T(8,128)(2,1)S(1)} %pad_maximum_fusion.1.refs_0_), channel_id=1, source_target_pairs={{32,0},{33,1},{64,32},{65,33},{96,64},{97,65},{128,96},{129,97},{1... | collective-permute-start | bytes 737288 | tf_op jit(solution)/shard_map/ppermute | solution.py:209
  55.4 1.9 %collective-permute-start.4 = (bf16[3,160,256]{2,1,0:T(8,128)(2,1)S(1)}, bf16[3,160,256]{2,1,0:T(8,128)(2,1)S(1)}, u32[]{:S(2)}, u32[]{:S(2)}) collective-permute-start(bf16[3,160,256]{2,1,0:T(8,128)(2,1)S(1)} %pad_maximum_fusion.1.refs_0_), channel_id=1, source_target_pairs={{480,0},{481,1},{0,32},{1,33},{32,64},{33,65},{64,96},{65,97},{96,... | collective-permute-start | bytes 737288 | tf_op jit(solution)/shard_map/ppermute | solution.py:209
  57.4 4.1 %collective-permute-start.2 = (bf16[160,256]{1,0:T(8,128)(2,1)S(1)}, bf16[160,256]{1,0:T(8,128)(2,1)S(1)}, u32[]{:S(2)}, u32[]{:S(2)}) collective-permute-start(bf16[160,256]{1,0:T(8,128)(2,1)S(1)} %broadcast_select_fusion), channel_id=1, source_target_pairs={{128,0},{385,1},{160,32},{417,33},{192,64},{449,65},{224,96},{481,... | collective-permute-start | bytes 245768 | tf_op jit(solution)/shard_map/ppermute | solution.py:209
  61.4 0.0 collective-permute-done.5
  61.5 0.2 maximum_select_fusion
  61.7 5.8 %shard_map.76 = (f32[4096,128]{1,0:T(8,128)S(1)}, f32[4096,128]{1,0:T(8,128)S(1)}) custom-call(bf16[3,160,256]{2,1,0:T(8,128)(2,1)S(1)} %pad_maximum_fusion.1.refs_0_, bf16[4096,256]{1,0:T(8,128)(2,1)S(1)} %bitcast.43), custom_call_target="tpu_custom_call" | custom-call | tf_op jit(solution)/shard_map/pallas_call | solution.py:158
  67.5 1.1 collective-permute-done.2
  68.6 0.0 collective-permute-done.3.refs_0_
  68.6 1.4 collective-permute-done.4.refs_1_
  70.0 1.9 %collective-permute-start.6 = (bf16[4,160,256]{2,1,0:T(8,128)(2,1)S(1)}, bf16[4,160,256]{2,1,0:T(8,128)(2,1)S(1)}, u32[]{:S(2)}, u32[]{:S(2)}) collective-permute-start(bf16[4,160,256]{2,1,0:T(8,128)(2,1)S(1)} %pad_maximum_fusion), channel_id=1, source_target_pairs={{64,0},{449,1},{96,32},{481,33},{128,64},{1,65},{160,96},{33,97},{... | collective-permute-start | bytes 983048 | tf_op jit(solution)/shard_map/ppermute | solution.py:209
  71.9 4.0 %collective-permute-start.7 = (bf16[1,160,256]{2,1,0:T(8,128)(2,1)S(1)}, bf16[1,160,256]{2,1,0:T(8,128)(2,1)S(1)}, u32[]{:S(2)}, u32[]{:S(2)}) collective-permute-start(bf16[1,160,256]{2,1,0:T(8,128)(2,1)S(1)} %bitcast.47), channel_id=1, source_target_pairs={{32,0},{33,1},{64,32},{65,33},{96,64},{97,65},{128,96},{129,97},{1... | collective-permute-start | bytes 245768 | tf_op jit(solution)/shard_map/ppermute | solution.py:209
  75.9 3.4 %collective-permute-start.8 = (bf16[1,160,256]{2,1,0:T(8,128)(2,1)S(1)}, bf16[1,160,256]{2,1,0:T(8,128)(2,1)S(1)}, u32[]{:S(2)}, u32[]{:S(2)}) collective-permute-start(bf16[1,160,256]{2,1,0:T(8,128)(2,1)S(1)} %bitcast.48), channel_id=1, source_target_pairs={{480,0},{481,1},{0,32},{1,33},{32,64},{33,65},{64,96},{65,97},{96,... | collective-permute-start | bytes 245768 | tf_op jit(solution)/shard_map/ppermute | solution.py:209
  79.3 7.8 %shard_map.77.refs_6_ = f32[4096,128]{1,0:T(8,128)S(1)} custom-call(bf16[3,160,256]{2,1,0:T(8,128)(2,1)S(1)} %collective-permute-done.3.refs_0_, bf16[3,160,256]{2,1,0:T(8,128)(2,1)S(1)} %collective-permute-done.4.refs_1_, bf16[4096,256]{1,0:T(8,128)(2,1)S(1)} %bitcast.44, f32[4096,128]{1,0:T(8,128)S(1)} %get-tuple-element.23.refs_3_.refs_5_, ...), custom_call_target="tpu_custom_call" | custom-call | tf_op jit(solution)/shard_map/pallas_call | solution.py:158
  87.1 0.0 copy-start
  87.1 0.0 copy-start.1
  87.2 0.0 copy-start.2
  87.2 0.0 collective-permute-done.7.refs_2_
  87.2 0.0 collective-permute-done.8.refs_3_
  87.2 0.0 collective-permute-done.6.refs_1_
  87.2 8.6 %shard_map.78 = bf16[32,4,2048]{2,1,0:T(4,128)(2,1)S(1)} custom-call(bf16[1,160,256]{2,1,0:T(8,128)(2,1)S(1)} %bitcast.49, bf16[4,160,256]{2,1,0:T(8,128)(2,1)S(1)} %collective-permute-done.6.refs_1_, bf16[1,160,256]{2,1,0:T(8,128)(2,1)S(1)} %collective-permute-done.7.refs_2_, bf16[1,160,256]{2,1,0:T(8,128)(2,1)S(1)} %collective-permute-done.8.refs_3_, ...), custom_call_target="tpu_custom_call" | custom-call | tf_op jit(solution)/shard_map/pallas_call | solution.py:158
  95.8 17.3 %all_to_all.34 = bf16[32,4,2048]{2,1,0:T(4,128)(2,1)S(1)} all-to-all(bf16[32,4,2048]{2,1,0:T(4,128)(2,1)S(1)} %shard_map.78), channel_id=1, replica_groups=mesh['z'=16,'ylo'=2,'yhi'=2,'x'=4,'core'=2] {'ylo','yhi','x','core'}, dimensions={0} | all-to-all | bytes 1048576 | tf_op jit(solution)/shard_map/all_to_all | solution.py:250
  113.1 0.2 convert_reduce_fusion
  113.4 0.0 copy-done
  113.4 0.0 copy-done.1
  113.4 0.2 multiply_reduce_fusion.2
  113.6 21.7 %all_to_all.35 = f32[32,4,4]{2,1,0:T(4,128)S(1)} all-to-all(f32[32,4,4]{2,1,0:T(4,128)S(1)} %broadcast_in_dim.8), channel_id=1, replica_groups=mesh['z'=16,'ylo'=2,'yhi'=2,'x'=4,'core'=2] {'z','ylo'}, dimensions={0} | all-to-all | bytes 4096 | tf_op jit(solution)/shard_map/all_to_all | solution.py:192
  135.4 0.0 copy-done.2
  135.4 0.7 multiply_add_fusion
  (9 shorter events, 0.2 us)
Async XLA Ops:
  2.0 13.7 %all-to-all-start = ((bf16[4,16,128]{2,0,1:T(4,128)(2,1)}), bf16[4,16,128]{2,0,1:T(4,128)(2,1)S(1)}, u32[]{:S(2)}, u32[]{:S(2)}) async-start(bf16[4,16,128]{2,0,1:T(4,128)(2,1)} %convert_bitcast_fusion), calls=%async_computation | async-start | bytes 32768 | tf_op jit(solution)/shard_map/all_to_all | solution.py:215
  16.8 29.6 %all-to-all-start.1 = ((bf16[16,128,256]{2,1,0:T(8,128)(2,1)}), bf16[16,128,256]{2,1,0:T(8,128)(2,1)S(1)}, u32[]{:S(2)}, u32[]{:S(2)}) async-start(bf16[16,128,256]{2,1,0:T(8,128)(2,1)} %broadcast_in_dim.6), calls=%async_computation.1 | async-start | bytes 2097152 | tf_op jit(solution)/shard_map/all_to_all | solution.py:192
  23.4 17.9 %collective-permute-start = (bf16[160,256]{1,0:T(8,128)(2,1)S(1)}, bf16[160,256]{1,0:T(8,128)(2,1)S(1)}, u32[]{:S(2)}, u32[]{:S(2)}) collective-permute-start(bf16[160,256]{1,0:T(8,128)(2,1)S(1)} %get-tuple-element.36), channel_id=1, source_target_pairs={{128,0},{129,1},{160,32},{161,33},{192,64},{193,65},{224,96},{225,... | collective-permute-start | bytes 245768 | tf_op jit(solution)/shard_map/ppermute | solution.py:209
  34.4 11.9 %collective-permute-start.1 = (bf16[160,256]{1,0:T(8,128)(2,1)S(1)}, bf16[160,256]{1,0:T(8,128)(2,1)S(1)}, u32[]{:S(2)}, u32[]{:S(2)}) collective-permute-start(bf16[160,256]{1,0:T(8,128)(2,1)S(1)} %get-tuple-element.36), channel_id=1, source_target_pairs={{384,0},{385,1},{416,32},{417,33},{448,64},{449,65},{480,96},{481,... | collective-permute-start | bytes 245768 | tf_op jit(solution)/shard_map/ppermute | solution.py:209
  46.4 15.1 %collective-permute-start.5 = (bf16[16,128,256]{2,1,0:T(8,128)(2,1)S(1)}, bf16[16,128,256]{2,1,0:T(8,128)(2,1)S(1)}, u32[]{:S(2)}, u32[]{:S(2)}) collective-permute-start(bf16[16,128,256]{2,1,0:T(8,128)(2,1)S(1)} %all-to-all-done.1), channel_id=1, source_target_pairs={{0,1},{1,0},{2,3},{3,2},{4,5},{5,4},{6,7},{7,6},{8,9},{9,8},{10,11... | collective-permute-start | bytes 3145736 | tf_op jit(solution)/shard_map/ppermute | solution.py:232
  48.3 20.3 %collective-permute-start.3 = (bf16[3,160,256]{2,1,0:T(8,128)(2,1)S(1)}, bf16[3,160,256]{2,1,0:T(8,128)(2,1)S(1)}, u32[]{:S(2)}, u32[]{:S(2)}) collective-permute-start(bf16[3,160,256]{2,1,0:T(8,128)(2,1)S(1)} %pad_maximum_fusion.1.refs_0_), channel_id=1, source_target_pairs={{32,0},{33,1},{64,32},{65,33},{96,64},{97,65},{128,96},{129,97},{1... | collective-permute-start | bytes 737288 | tf_op jit(solution)/shard_map/ppermute | solution.py:209
  55.4 14.5 %collective-permute-start.4 = (bf16[3,160,256]{2,1,0:T(8,128)(2,1)S(1)}, bf16[3,160,256]{2,1,0:T(8,128)(2,1)S(1)}, u32[]{:S(2)}, u32[]{:S(2)}) collective-permute-start(bf16[3,160,256]{2,1,0:T(8,128)(2,1)S(1)} %pad_maximum_fusion.1.refs_0_), channel_id=1, source_target_pairs={{480,0},{481,1},{0,32},{1,33},{32,64},{33,65},{64,96},{65,97},{96,... | collective-permute-start | bytes 737288 | tf_op jit(solution)/shard_map/ppermute | solution.py:209
  57.4 11.2 %collective-permute-start.2 = (bf16[160,256]{1,0:T(8,128)(2,1)S(1)}, bf16[160,256]{1,0:T(8,128)(2,1)S(1)}, u32[]{:S(2)}, u32[]{:S(2)}) collective-permute-start(bf16[160,256]{1,0:T(8,128)(2,1)S(1)} %broadcast_select_fusion), channel_id=1, source_target_pairs={{128,0},{385,1},{160,32},{417,33},{192,64},{449,65},{224,96},{481,... | collective-permute-start | bytes 245768 | tf_op jit(solution)/shard_map/ppermute | solution.py:209
  70.0 17.2 %collective-permute-start.6 = (bf16[4,160,256]{2,1,0:T(8,128)(2,1)S(1)}, bf16[4,160,256]{2,1,0:T(8,128)(2,1)S(1)}, u32[]{:S(2)}, u32[]{:S(2)}) collective-permute-start(bf16[4,160,256]{2,1,0:T(8,128)(2,1)S(1)} %pad_maximum_fusion), channel_id=1, source_target_pairs={{64,0},{449,1},{96,32},{481,33},{128,64},{1,65},{160,96},{33,97},{... | collective-permute-start | bytes 983048 | tf_op jit(solution)/shard_map/ppermute | solution.py:209
  71.9 15.2 %collective-permute-start.7 = (bf16[1,160,256]{2,1,0:T(8,128)(2,1)S(1)}, bf16[1,160,256]{2,1,0:T(8,128)(2,1)S(1)}, u32[]{:S(2)}, u32[]{:S(2)}) collective-permute-start(bf16[1,160,256]{2,1,0:T(8,128)(2,1)S(1)} %bitcast.47), channel_id=1, source_target_pairs={{32,0},{33,1},{64,32},{65,33},{96,64},{97,65},{128,96},{129,97},{1... | collective-permute-start | bytes 245768 | tf_op jit(solution)/shard_map/ppermute | solution.py:209
  75.9 11.2 %collective-permute-start.8 = (bf16[1,160,256]{2,1,0:T(8,128)(2,1)S(1)}, bf16[1,160,256]{2,1,0:T(8,128)(2,1)S(1)}, u32[]{:S(2)}, u32[]{:S(2)}) collective-permute-start(bf16[1,160,256]{2,1,0:T(8,128)(2,1)S(1)} %bitcast.48), channel_id=1, source_target_pairs={{480,0},{481,1},{0,32},{1,33},{32,64},{33,65},{64,96},{65,97},{96,... | collective-permute-start | bytes 245768 | tf_op jit(solution)/shard_map/ppermute | solution.py:209
  87.1 26.2 %copy-start = (f32[4,2048]{1,0:T(4,128)S(1)}, f32[4,2048]{1,0:T(4,128)}, u32[]{:S(2)}) copy-start(f32[4,2048]{1,0:T(4,128)} %param.9) | copy-start | bytes 98308
  87.1 26.2 %copy-start.1 = (f32[4,2048]{1,0:T(4,128)S(1)}, f32[4,2048]{1,0:T(4,128)}, u32[]{:S(2)}) copy-start(f32[4,2048]{1,0:T(4,128)} %param.8) | copy-start | bytes 98308
  87.2 48.2 %copy-start.2 = (f32[4,2048]{1,0:T(4,128)S(1)}, f32[4,2048]{1,0:T(4,128)}, u32[]{:S(2)}) copy-start(f32[4,2048]{1,0:T(4,128)} %param.7) | copy-start | bytes 98308

commit v2 on v1

--- a/solution.py
+++ b/solution.py
@@ -20,7 +20,6 @@
 BLOCK = ("z", "ylo")
 PROBE = ("yhi", "x", "core")
 PLANE = ("ylo", "yhi", "x", "core")
-CHIPS = ("ylo", "yhi", "x")
 
 FEAT = 256
 PROBES = 64
@@ -188,14 +187,12 @@
     return product_call(next_kernel, sources, [cols, col_norms, carry], n_cols, out_shape)
 
 
-def to_all(own, axes):
-    return lax.all_to_all(
-        jnp.broadcast_to(own[None], (lax.axis_size(axes),) + own.shape),
-        axes,
-        split_axis=0,
-        concat_axis=0,
-        tiled=True,
-    )
+def copies(own, axes):
+    return jnp.broadcast_to(own[None], (lax.axis_size(axes),) + own.shape)
+
+
+def exchanged(pieces, axes):
+    return lax.all_to_all(pieces, axes, split_axis=0, concat_axis=0, tiled=True)
 
 
 def from_z(shard, by, core_by=None):
@@ -213,28 +210,21 @@
     own_rows = (points.astype(jnp.float32) * inv_length[None, :]).astype(jnp.bfloat16)
     low_direction = direction.astype(jnp.bfloat16)
     own_dirs = lax.all_to_all(low_direction, PROBE, split_axis=1, concat_axis=0, tiled=True)
-    plane_rows, own_dirs = lax.optimization_barrier((own_rows, own_dirs))
+    plane_copies, own_dirs = lax.optimization_barrier((copies(own_rows, PLANE), own_dirs))
     half = PROBES // 2
     packed = jnp.concatenate(
         [own_rows, jnp.concatenate([own_dirs[:half], own_dirs[half:]], axis=1)], axis=0
     )
     first_core = lax.axis_index("core") == 0
 
-    own_half = to_all(plane_rows, CHIPS)
+    cols = exchanged(plane_copies, PLANE).reshape(-1, FEAT)
 
     ahead = from_z(packed, 4)
     behind = from_z(packed, -4)
-    own_half, ahead, behind = lax.optimization_barrier((own_half, ahead, behind))
     far = jnp.stack([packed, ahead, behind])
     above = from_z(far, 1)
     below = from_z(far, -1)
     opposite = from_z(jnp.where(first_core, ahead, behind), 4, -4)
-    other_half = lax.ppermute(own_half, "core", [(0, 1), (1, 0)])
-    cols = jnp.where(
-        first_core,
-        jnp.stack([own_half, other_half], axis=1),
-        jnp.stack([other_half, own_half], axis=1),
-    ).reshape(-1, FEAT)
     partial_value, col_norms = first_product([far], cols)
 
     far, opposite, above, below, partial_value = lax.optimization_barrier(
@@ -247,7 +237,7 @@
     partial_value = tile_product(
         [opposite, second, last_above, last_below], cols, col_norms, partial_value, last=True
     )
-    pieces = lax.all_to_all(partial_value, PLANE, split_axis=0, concat_axis=0, tiled=True)
+    pieces = exchanged(partial_value, PLANE)
     image = jnp.sum(pieces.astype(jnp.float32), axis=0) + noise_var * low_direction.astype(
         jnp.float32
     )
@@ -259,7 +249,7 @@
             jnp.sum(image * image, axis=1),
         ]
     )
-    sums = jnp.sum(to_all(sums, BLOCK), axis=0)
+    sums = jnp.sum(exchanged(copies(sums, BLOCK), BLOCK), axis=0)
     old_norm, curvature, cross, image_norm = sums[0], sums[1], sums[2], sums[3]
     step_len = old_norm / curvature
     new_norm = jnp.maximum(old_norm - step_len * (2.0 * cross - step_len * image_norm), 0.0)

time: 137 us -> 136 us (level)
    ppermute x1 -> x0, starting transfers between devices: 1.91 us -> none  [shards(): other_half = lax.ppermute(own_half, 'core', [(0, 1), (1, 0)])]
  transfers between devices with their start and end apart: 11 -> 10, of which waited for: 5 -> 5; matrix products, arithmetic and copies ran while one was open for 1% -> 1% of each run, Pallas kernels for 10% -> 10%
where the time goes in v2:
time: 136 us; the launch traced here: 135 us
  starting transfers between devices  49.4 us (36%)
  blocking collectives  38.8 us (29%)
  Pallas kernels  22.3 us (16%)
  waiting for transfers between devices  18.6 us (14%)
  other arithmetic  3.5 us (3%)
  local copies, waits for them, and re-layouts  1.6 us (1%)
    all_to_all x2, blocking collectives, exchanged(): return lax.all_to_all(pieces, axes, split_axis=0, concat_axis=0, tiled=True)  38.8 us
    ppermute x8, starting transfers between devices, from_z(): return lax.ppermute(shard, ('z', 'core'), pairs)  36.4 us
    pallas_call x3, Pallas kernels, product_call(): pl.pallas_call(functools.partial(kernel, len(sources)), in_specs=[WHOLE]...  22.3 us
    ppermute x8, waiting for transfers between devices, from_z(): return lax.ppermute(shard, ('z', 'core'), pairs)  11.9 us
    all_to_all x1, starting transfers between devices, exchanged(): return lax.all_to_all(pieces, axes, split_axis=0, concat_axis=0, tiled=True)  6.9 us
    all_to_all x1, waiting for transfers between devices, shards(): lax.all_to_all(low_direction, PROBE, split_axis=1, concat_axis=0, tiled=T...  6.72 us
    all_to_all x1, starting transfers between devices, shards(): lax.all_to_all(low_direction, PROBE, split_axis=1, concat_axis=0, tiled=T...  6.14 us
  transfers between devices with their start and end apart: 10, of which 5 were waited for; matrix products, arithmetic and copies ran while one was open for 1% of the time, Pallas kernels for 10%

profile of v2, /device:TPU:8, one launch (start us, length us, event | category | flops | bytes accessed | tf_op | source)
XLA Modules:
  0.0 135.0 jit_solution(11113789922109321465)
XLA Ops:
  0.6 1.4 %convert_bitcast_fusion = bf16[4,16,128]{2,0,1:T(4,128)(2,1)} fusion(f32[4,2048]{1,0:T(4,128)} %param.9), kind=kLoop, calls=%fused_computation.14 | loop fusion | flops 8192 | bytes 49152 | tf_op jit(solution)/shard_map/all_to_all | solution.py:212
  2.0 6.1 %all-to-all-start = ((bf16[4,16,128]{2,0,1:T(4,128)(2,1)}), bf16[4,16,128]{2,0,1:T(4,128)(2,1)S(1)}, u32[]{:S(2)}, u32[]{:S(2)}) async-start(bf16[4,16,128]{2,0,1:T(4,128)(2,1)} %convert_bitcast_fusion), calls=%async_computation | async-start | bytes 32768 | tf_op jit(solution)/shard_map/all_to_all | solution.py:212
  8.1 0.9 multiply_convert_fusion
  9.0 6.7 %all-to-all-done = bf16[4,16,128]{2,0,1:T(4,128)(2,1)S(1)} async-done(((bf16[4,16,128]{2,0,1:T(4,128)(2,1)}), bf16[4,16,128]{2,0,1:T(4,128)(2,1)S(1)}, u32[]{:S(2)}, u32[]{:S(2)}) %all-to-all-start) | async-done | bytes 16416 | tf_op jit(solution)/shard_map/all_to_all | solution.py:212
  15.7 1.6 %broadcast_in_dim.6 = bf16[32,128,256]{2,1,0:T(8,128)(2,1)} broadcast(bf16[128,256]{1,0:T(8,128)(2,1)S(1)} %multiply_convert_fusion), dimensions={1,2} | broadcast | bytes 2162688 | tf_op jit(solution)/shard_map/broadcast_in_dim | solution.py:191
  17.3 6.9 %all-to-all-start.1 = ((bf16[32,128,256]{2,1,0:T(8,128)(2,1)}), bf16[32,128,256]{2,1,0:T(8,128)(2,1)S(1)}, u32[]{:S(2)}, u32[]{:S(2)}) async-start(bf16[32,128,256]{2,1,0:T(8,128)(2,1)} %broadcast_in_dim.6), calls=%async_computation.1 | async-start | bytes 4194304 | tf_op jit(solution)/shard_map/all_to_all | solution.py:195
  24.2 11.0 %collective-permute-start = (bf16[160,256]{1,0:T(8,128)(2,1)S(1)}, bf16[160,256]{1,0:T(8,128)(2,1)S(1)}, u32[]{:S(2)}, u32[]{:S(2)}) collective-permute-start(bf16[160,256]{1,0:T(8,128)(2,1)S(1)} %get-tuple-element.30), channel_id=1, source_target_pairs={{128,0},{129,1},{160,32},{161,33},{192,64},{193,65},{224,96},{225,... | collective-permute-start | bytes 245768 | tf_op jit(solution)/shard_map/ppermute | solution.py:206
  35.2 1.9 %collective-permute-start.1 = (bf16[160,256]{1,0:T(8,128)(2,1)S(1)}, bf16[160,256]{1,0:T(8,128)(2,1)S(1)}, u32[]{:S(2)}, u32[]{:S(2)}) collective-permute-start(bf16[160,256]{1,0:T(8,128)(2,1)S(1)} %get-tuple-element.30), channel_id=1, source_target_pairs={{384,0},{385,1},{416,32},{417,33},{448,64},{449,65},{480,96},{481,... | collective-permute-start | bytes 245768 | tf_op jit(solution)/shard_map/ppermute | solution.py:206
  37.1 5.4 %collective-permute-done = bf16[160,256]{1,0:T(8,128)(2,1)S(1)} collective-permute-done((bf16[160,256]{1,0:T(8,128)(2,1)S(1)}, bf16[160,256]{1,0:T(8,128)(2,1)S(1)}, u32[]{:S(2)}, u32[]{:S(2)}) %collective-permute-start) | collective-permute-done | bytes 81952 | tf_op jit(solution)/shard_map/ppermute | solution.py:206
  42.5 4.6 %collective-permute-done.1 = bf16[160,256]{1,0:T(8,128)(2,1)S(1)} collective-permute-done((bf16[160,256]{1,0:T(8,128)(2,1)S(1)}, bf16[160,256]{1,0:T(8,128)(2,1)S(1)}, u32[]{:S(2)}, u32[]{:S(2)}) %collective-permute-start.1) | collective-permute-done | bytes 81952 | tf_op jit(solution)/shard_map/ppermute | solution.py:206
  47.2 7.4 %collective-permute-start.3 = (bf16[3,160,256]{2,1,0:T(8,128)(2,1)S(1)}, bf16[3,160,256]{2,1,0:T(8,128)(2,1)S(1)}, u32[]{:S(2)}, u32[]{:S(2)}) collective-permute-start(bf16[3,160,256]{2,1,0:T(8,128)(2,1)S(1)} %pad_maximum_fusion.1.refs_0_), channel_id=1, source_target_pairs={{32,0},{33,1},{64,32},{65,33},{96,64},{97,65},{128,96},{129,97},{1... | collective-permute-start | bytes 737288 | tf_op jit(solution)/shard_map/ppermute | solution.py:206
  54.6 1.9 %collective-permute-start.4 = (bf16[3,160,256]{2,1,0:T(8,128)(2,1)S(1)}, bf16[3,160,256]{2,1,0:T(8,128)(2,1)S(1)}, u32[]{:S(2)}, u32[]{:S(2)}) collective-permute-start(bf16[3,160,256]{2,1,0:T(8,128)(2,1)S(1)} %pad_maximum_fusion.1.refs_0_), channel_id=1, source_target_pairs={{480,0},{481,1},{0,32},{1,33},{32,64},{33,65},{64,96},{65,97},{96,... | collective-permute-start | bytes 737288 | tf_op jit(solution)/shard_map/ppermute | solution.py:206
  56.6 4.1 %collective-permute-start.2 = (bf16[160,256]{1,0:T(8,128)(2,1)S(1)}, bf16[160,256]{1,0:T(8,128)(2,1)S(1)}, u32[]{:S(2)}, u32[]{:S(2)}) collective-permute-start(bf16[160,256]{1,0:T(8,128)(2,1)S(1)} %broadcast_select_fusion), channel_id=1, source_target_pairs={{128,0},{385,1},{160,32},{417,33},{192,64},{449,65},{224,96},{481,... | collective-permute-start | bytes 245768 | tf_op jit(solution)/shard_map/ppermute | solution.py:206
  60.6 0.0 all-to-all-done.1
  60.6 5.8 %shard_map.76 = (f32[4096,128]{1,0:T(8,128)S(1)}, f32[4096,128]{1,0:T(8,128)S(1)}) custom-call(bf16[3,160,256]{2,1,0:T(8,128)(2,1)S(1)} %pad_maximum_fusion.1.refs_0_, bf16[4096,256]{1,0:T(8,128)(2,1)S(1)} %bitcast.41), custom_call_target="tpu_custom_call" | custom-call | tf_op jit(solution)/shard_map/pallas_call | solution.py:157
  66.5 1.3 collective-permute-done.2
  67.8 0.0 collective-permute-done.3.refs_0_
  67.8 0.6 collective-permute-done.4.refs_1_
  68.4 1.9 %collective-permute-start.5 = (bf16[4,160,256]{2,1,0:T(8,128)(2,1)S(1)}, bf16[4,160,256]{2,1,0:T(8,128)(2,1)S(1)}, u32[]{:S(2)}, u32[]{:S(2)}) collective-permute-start(bf16[4,160,256]{2,1,0:T(8,128)(2,1)S(1)} %pad_maximum_fusion), channel_id=1, source_target_pairs={{64,0},{449,1},{96,32},{481,33},{128,64},{1,65},{160,96},{33,97},{... | collective-permute-start | bytes 983048 | tf_op jit(solution)/shard_map/ppermute | solution.py:206
  70.3 4.8 %collective-permute-start.6 = (bf16[1,160,256]{2,1,0:T(8,128)(2,1)S(1)}, bf16[1,160,256]{2,1,0:T(8,128)(2,1)S(1)}, u32[]{:S(2)}, u32[]{:S(2)}) collective-permute-start(bf16[1,160,256]{2,1,0:T(8,128)(2,1)S(1)} %bitcast.45), channel_id=1, source_target_pairs={{32,0},{33,1},{64,32},{65,33},{96,64},{97,65},{128,96},{129,97},{1... | collective-permute-start | bytes 245768 | tf_op jit(solution)/shard_map/ppermute | solution.py:206
  75.1 3.4 %collective-permute-start.7 = (bf16[1,160,256]{2,1,0:T(8,128)(2,1)S(1)}, bf16[1,160,256]{2,1,0:T(8,128)(2,1)S(1)}, u32[]{:S(2)}, u32[]{:S(2)}) collective-permute-start(bf16[1,160,256]{2,1,0:T(8,128)(2,1)S(1)} %bitcast.46), channel_id=1, source_target_pairs={{480,0},{481,1},{0,32},{1,33},{32,64},{33,65},{64,96},{65,97},{96,... | collective-permute-start | bytes 245768 | tf_op jit(solution)/shard_map/ppermute | solution.py:206
  78.5 7.8 %shard_map.77.refs_6_ = f32[4096,128]{1,0:T(8,128)S(1)} custom-call(bf16[3,160,256]{2,1,0:T(8,128)(2,1)S(1)} %collective-permute-done.3.refs_0_, bf16[3,160,256]{2,1,0:T(8,128)(2,1)S(1)} %collective-permute-done.4.refs_1_, bf16[4096,256]{1,0:T(8,128)(2,1)S(1)} %bitcast.42, f32[4096,128]{1,0:T(8,128)S(1)} %get-tuple-element.17.refs_3_.refs_5_, ...), custom_call_target="tpu_custom_call" | custom-call | tf_op jit(solution)/shard_map/pallas_call | solution.py:157
  86.3 0.0 copy-start
  86.3 0.0 copy-start.1
  86.3 0.0 copy-start.2
  86.3 0.0 collective-permute-done.6.refs_2_
  86.4 0.0 collective-permute-done.7.refs_3_
  86.4 0.0 collective-permute-done.5.refs_1_
  86.4 8.6 %shard_map.78 = bf16[32,4,2048]{2,1,0:T(4,128)(2,1)S(1)} custom-call(bf16[1,160,256]{2,1,0:T(8,128)(2,1)S(1)} %bitcast.47, bf16[4,160,256]{2,1,0:T(8,128)(2,1)S(1)} %collective-permute-done.5.refs_1_, bf16[1,160,256]{2,1,0:T(8,128)(2,1)S(1)} %collective-permute-done.6.refs_2_, bf16[1,160,256]{2,1,0:T(8,128)(2,1)S(1)} %collective-permute-done.7.refs_3_, ...), custom_call_target="tpu_custom_call" | custom-call | tf_op jit(solution)/shard_map/pallas_call | solution.py:157
  95.0 17.3 %all_to_all.34 = bf16[32,4,2048]{2,1,0:T(4,128)(2,1)S(1)} all-to-all(bf16[32,4,2048]{2,1,0:T(4,128)(2,1)S(1)} %shard_map.78), channel_id=1, replica_groups=mesh['z'=16,'ylo'=2,'yhi'=2,'x'=4,'core'=2] {'ylo','yhi','x','core'}, dimensions={0} | all-to-all | bytes 1048576 | tf_op jit(solution)/shard_map/all_to_all | solution.py:195
  112.3 0.2 convert_reduce_fusion
  112.5 0.0 copy-done
  112.5 0.0 copy-done.1
  112.5 0.2 multiply_reduce_fusion.2
  112.7 21.5 %all_to_all.35 = f32[32,4,4]{2,1,0:T(4,128)S(1)} all-to-all(f32[32,4,4]{2,1,0:T(4,128)S(1)} %broadcast_in_dim.8), channel_id=1, replica_groups=mesh['z'=16,'ylo'=2,'yhi'=2,'x'=4,'core'=2] {'z','ylo'}, dimensions={0} | all-to-all | bytes 4096 | tf_op jit(solution)/shard_map/all_to_all | solution.py:195
  134.3 0.0 copy-done.2
  134.3 0.7 multiply_add_fusion
  (9 shorter events, 0.2 us)
Async XLA Ops:
  2.0 13.7 %all-to-all-start = ((bf16[4,16,128]{2,0,1:T(4,128)(2,1)}), bf16[4,16,128]{2,0,1:T(4,128)(2,1)S(1)}, u32[]{:S(2)}, u32[]{:S(2)}) async-start(bf16[4,16,128]{2,0,1:T(4,128)(2,1)} %convert_bitcast_fusion), calls=%async_computation | async-start | bytes 32768 | tf_op jit(solution)/shard_map/all_to_all | solution.py:212
  17.3 43.3 %all-to-all-start.1 = ((bf16[32,128,256]{2,1,0:T(8,128)(2,1)}), bf16[32,128,256]{2,1,0:T(8,128)(2,1)S(1)}, u32[]{:S(2)}, u32[]{:S(2)}) async-start(bf16[32,128,256]{2,1,0:T(8,128)(2,1)} %broadcast_in_dim.6), calls=%async_computation.1 | async-start | bytes 4194304 | tf_op jit(solution)/shard_map/all_to_all | solution.py:195
  24.2 18.3 %collective-permute-start = (bf16[160,256]{1,0:T(8,128)(2,1)S(1)}, bf16[160,256]{1,0:T(8,128)(2,1)S(1)}, u32[]{:S(2)}, u32[]{:S(2)}) collective-permute-start(bf16[160,256]{1,0:T(8,128)(2,1)S(1)} %get-tuple-element.30), channel_id=1, source_target_pairs={{128,0},{129,1},{160,32},{161,33},{192,64},{193,65},{224,96},{225,... | collective-permute-start | bytes 245768 | tf_op jit(solution)/shard_map/ppermute | solution.py:206
  35.2 11.9 %collective-permute-start.1 = (bf16[160,256]{1,0:T(8,128)(2,1)S(1)}, bf16[160,256]{1,0:T(8,128)(2,1)S(1)}, u32[]{:S(2)}, u32[]{:S(2)}) collective-permute-start(bf16[160,256]{1,0:T(8,128)(2,1)S(1)} %get-tuple-element.30), channel_id=1, source_target_pairs={{384,0},{385,1},{416,32},{417,33},{448,64},{449,65},{480,96},{481,... | collective-permute-start | bytes 245768 | tf_op jit(solution)/shard_map/ppermute | solution.py:206
  47.2 20.6 %collective-permute-start.3 = (bf16[3,160,256]{2,1,0:T(8,128)(2,1)S(1)}, bf16[3,160,256]{2,1,0:T(8,128)(2,1)S(1)}, u32[]{:S(2)}, u32[]{:S(2)}) collective-permute-start(bf16[3,160,256]{2,1,0:T(8,128)(2,1)S(1)} %pad_maximum_fusion.1.refs_0_), channel_id=1, source_target_pairs={{32,0},{33,1},{64,32},{65,33},{96,64},{97,65},{128,96},{129,97},{1... | collective-permute-start | bytes 737288 | tf_op jit(solution)/shard_map/ppermute | solution.py:206
  54.6 13.8 %collective-permute-start.4 = (bf16[3,160,256]{2,1,0:T(8,128)(2,1)S(1)}, bf16[3,160,256]{2,1,0:T(8,128)(2,1)S(1)}, u32[]{:S(2)}, u32[]{:S(2)}) collective-permute-start(bf16[3,160,256]{2,1,0:T(8,128)(2,1)S(1)} %pad_maximum_fusion.1.refs_0_), channel_id=1, source_target_pairs={{480,0},{481,1},{0,32},{1,33},{32,64},{33,65},{64,96},{65,97},{96,... | collective-permute-start | bytes 737288 | tf_op jit(solution)/shard_map/ppermute | solution.py:206
  56.6 11.2 %collective-permute-start.2 = (bf16[160,256]{1,0:T(8,128)(2,1)S(1)}, bf16[160,256]{1,0:T(8,128)(2,1)S(1)}, u32[]{:S(2)}, u32[]{:S(2)}) collective-permute-start(bf16[160,256]{1,0:T(8,128)(2,1)S(1)} %broadcast_select_fusion), channel_id=1, source_target_pairs={{128,0},{385,1},{160,32},{417,33},{192,64},{449,65},{224,96},{481,... | collective-permute-start | bytes 245768 | tf_op jit(solution)/shard_map/ppermute | solution.py:206
  68.4 18.0 %collective-permute-start.5 = (bf16[4,160,256]{2,1,0:T(8,128)(2,1)S(1)}, bf16[4,160,256]{2,1,0:T(8,128)(2,1)S(1)}, u32[]{:S(2)}, u32[]{:S(2)}) collective-permute-start(bf16[4,160,256]{2,1,0:T(8,128)(2,1)S(1)} %pad_maximum_fusion), channel_id=1, source_target_pairs={{64,0},{449,1},{96,32},{481,33},{128,64},{1,65},{160,96},{33,97},{... | collective-permute-start | bytes 983048 | tf_op jit(solution)/shard_map/ppermute | solution.py:206
  70.3 16.0 %collective-permute-start.6 = (bf16[1,160,256]{2,1,0:T(8,128)(2,1)S(1)}, bf16[1,160,256]{2,1,0:T(8,128)(2,1)S(1)}, u32[]{:S(2)}, u32[]{:S(2)}) collective-permute-start(bf16[1,160,256]{2,1,0:T(8,128)(2,1)S(1)} %bitcast.45), channel_id=1, source_target_pairs={{32,0},{33,1},{64,32},{65,33},{96,64},{97,65},{128,96},{129,97},{1... | collective-permute-start | bytes 245768 | tf_op jit(solution)/shard_map/ppermute | solution.py:206
  75.1 11.2 %collective-permute-start.7 = (bf16[1,160,256]{2,1,0:T(8,128)(2,1)S(1)}, bf16[1,160,256]{2,1,0:T(8,128)(2,1)S(1)}, u32[]{:S(2)}, u32[]{:S(2)}) collective-permute-start(bf16[1,160,256]{2,1,0:T(8,128)(2,1)S(1)} %bitcast.46), channel_id=1, source_target_pairs={{480,0},{481,1},{0,32},{1,33},{32,64},{33,65},{64,96},{65,97},{96,... | collective-permute-start | bytes 245768 | tf_op jit(solution)/shard_map/ppermute | solution.py:206
  86.3 26.2 %copy-start = (f32[4,2048]{1,0:T(4,128)S(1)}, f32[4,2048]{1,0:T(4,128)}, u32[]{:S(2)}) copy-start(f32[4,2048]{1,0:T(4,128)} %param.9) | copy-start | bytes 98308
  86.3 26.2 %copy-start.1 = (f32[4,2048]{1,0:T(4,128)S(1)}, f32[4,2048]{1,0:T(4,128)}, u32[]{:S(2)}) copy-start(f32[4,2048]{1,0:T(4,128)} %param.8) | copy-start | bytes 98308
  86.3 48.0 %copy-start.2 = (f32[4,2048]{1,0:T(4,128)S(1)}, f32[4,2048]{1,0:T(4,128)}, u32[]{:S(2)}) copy-start(f32[4,2048]{1,0:T(4,128)} %param.7) | copy-start | bytes 98308

commit v3 on v2

--- a/solution.py
+++ b/solution.py
@@ -206,11 +206,32 @@
     return lax.ppermute(shard, ("z", "core"), pairs)
 
 
+def scale_kernel(points_ref, inverse_ref, rows_ref, copies_ref):
+    rows = (points_ref[...].astype(jnp.float32) * inverse_ref[...]).astype(jnp.bfloat16)
+    rows_ref[...] = rows
+
+    @pl.loop(0, copies_ref.shape[0])
+    def _(at):
+        copies_ref[at] = rows
+
+
+def scaled_with_copies(points, inv_length, n_copies):
+    return pl.pallas_call(
+        scale_kernel,
+        in_specs=[WHOLE, WHOLE],
+        out_specs=[WHOLE, WHOLE],
+        out_shape=[
+            jax.ShapeDtypeStruct(points.shape, jnp.bfloat16),
+            jax.ShapeDtypeStruct((n_copies,) + points.shape, jnp.bfloat16),
+        ],
+    )(points, inv_length[None, :])
+
+
 def shards(points, inv_length, solution, residual, direction):
-    own_rows = (points.astype(jnp.float32) * inv_length[None, :]).astype(jnp.bfloat16)
+    own_rows, plane_copies = scaled_with_copies(points, inv_length, lax.axis_size(PLANE))
     low_direction = direction.astype(jnp.bfloat16)
     own_dirs = lax.all_to_all(low_direction, PROBE, split_axis=1, concat_axis=0, tiled=True)
-    plane_copies, own_dirs = lax.optimization_barrier((copies(own_rows, PLANE), own_dirs))
+    plane_copies, own_dirs = lax.optimization_barrier((plane_copies, own_dirs))
     half = PROBES // 2
     packed = jnp.concatenate(
         [own_rows, jnp.concatenate([own_dirs[:half], own_dirs[half:]], axis=1)], axis=0

time: 136 us -> 134 us (0.985)
  Pallas kernels: 22.3 us -> 24.7 us
  local copies, waits for them, and re-layouts: 1.6 us -> 0.04 us
  waiting for transfers between devices: 18.6 us -> 17.1 us
    pallas_call x0 -> x1, Pallas kernels: none -> 2.4 us  [scaled_with_copies(): pl.pallas_call(scale_kernel, in_specs=[WHOLE, WHOLE], out_specs=[WHOLE, W...]
    broadcast_in_dim x2 -> x1, local copies, waits for them, and re-layouts: 1.58 us -> 0.01 us  [copies(): return jnp.broadcast_to(own[None], (lax.axis_size(axes),) + own.shape)]
    all_to_all x1, waiting for transfers between devices: 6.72 us -> 5.19 us  [shards(): lax.all_to_all(low_direction, PROBE, split_axis=1, concat_axis=0, tiled=T...]
  transfers between devices with their start and end apart: 10 -> 10, of which waited for: 5 -> 5; matrix products, arithmetic and copies ran while one was open for 1% -> 0% of each run, Pallas kernels for 10% -> 12%
where the time goes in v3:
time: 134 us
  starting transfers between devices  49.5 us (37%)
  blocking collectives  38.8 us (29%)
  Pallas kernels  24.7 us (18%)
  waiting for transfers between devices  17.1 us (13%)
  other arithmetic  2.64 us (2%)
    all_to_all x2, blocking collectives, exchanged(): return lax.all_to_all(pieces, axes, split_axis=0, concat_axis=0, tiled=True)  38.8 us
    ppermute x8, starting transfers between devices, from_z(): return lax.ppermute(shard, ('z', 'core'), pairs)  36.4 us
    pallas_call x3, Pallas kernels, product_call(): pl.pallas_call(functools.partial(kernel, len(sources)), in_specs=[WHOLE]...  22.3 us
    ppermute x8, waiting for transfers between devices, from_z(): return lax.ppermute(shard, ('z', 'core'), pairs)  11.9 us
    all_to_all x1, starting transfers between devices, exchanged(): return lax.all_to_all(pieces, axes, split_axis=0, concat_axis=0, tiled=True)  7.03 us
    all_to_all x1, starting transfers between devices, shards(): lax.all_to_all(low_direction, PROBE, split_axis=1, concat_axis=0, tiled=T...  6.14 us
    all_to_all x1, waiting for transfers between devices, shards(): lax.all_to_all(low_direction, PROBE, split_axis=1, concat_axis=0, tiled=T...  5.19 us
  transfers between devices with their start and end apart: 10, of which 5 were waited for; matrix products, arithmetic and copies ran while one was open for 0% of the time, Pallas kernels for 12%

profile of v3, /device:TPU:8, one launch (start us, length us, event | category | flops | bytes accessed | tf_op | source)
XLA Modules:
  0.0 133.6 jit_solution(5176398184901314998)
XLA Ops:
  0.6 1.4 %convert_bitcast_fusion = bf16[4,16,128]{2,0,1:T(4,128)(2,1)} fusion(f32[4,2048]{1,0:T(4,128)} %param.9), kind=kLoop, calls=%fused_computation.13 | loop fusion | flops 8192 | bytes 49152 | tf_op jit(solution)/shard_map/all_to_all | solution.py:233
  2.0 6.1 %all-to-all-start = ((bf16[4,16,128]{2,0,1:T(4,128)(2,1)}), bf16[4,16,128]{2,0,1:T(4,128)(2,1)S(1)}, u32[]{:S(2)}, u32[]{:S(2)}) async-start(bf16[4,16,128]{2,0,1:T(4,128)(2,1)} %convert_bitcast_fusion), calls=%async_computation | async-start | bytes 32768 | tf_op jit(solution)/shard_map/all_to_all | solution.py:233
  8.1 2.4 %shard_map.76 = (bf16[128,256]{1,0:T(8,128)(2,1)}, bf16[32,128,256]{2,1,0:T(8,128)(2,1)}) custom-call(bf16[128,256]{1,0:T(8,128)(2,1)} %points_ref.1, f32[1,256]{1,0:T(1,128)} %bitcast.56), custom_call_target="tpu_custom_call" | custom-call | tf_op jit(solution)/shard_map/pallas_call | solution.py:219
  10.5 5.2 %all-to-all-done = bf16[4,16,128]{2,0,1:T(4,128)(2,1)S(1)} async-done(((bf16[4,16,128]{2,0,1:T(4,128)(2,1)}), bf16[4,16,128]{2,0,1:T(4,128)(2,1)S(1)}, u32[]{:S(2)}, u32[]{:S(2)}) %all-to-all-start) | async-done | bytes 16416 | tf_op jit(solution)/shard_map/all_to_all | solution.py:233
  15.7 0.0 copy-start.2
  15.7 7.0 %all-to-all-start.1 = ((bf16[32,128,256]{2,1,0:T(8,128)(2,1)}), bf16[32,128,256]{2,1,0:T(8,128)(2,1)S(1)}, u32[]{:S(2)}, u32[]{:S(2)}) async-start(bf16[32,128,256]{2,1,0:T(8,128)(2,1)} %get-tuple-element.17), calls=%async_computation.1 | async-start | bytes 4194304 | tf_op jit(solution)/shard_map/all_to_all | solution.py:195
  22.8 0.0 copy-done.2
  22.8 11.0 %collective-permute-start = (bf16[160,256]{1,0:T(8,128)(2,1)S(1)}, bf16[160,256]{1,0:T(8,128)(2,1)S(1)}, u32[]{:S(2)}, u32[]{:S(2)}) collective-permute-start(bf16[160,256]{1,0:T(8,128)(2,1)S(1)} %get-tuple-element.34), channel_id=1, source_target_pairs={{128,0},{129,1},{160,32},{161,33},{192,64},{193,65},{224,96},{225,... | collective-permute-start | bytes 245768 | tf_op jit(solution)/shard_map/ppermute | solution.py:206
  33.8 1.9 %collective-permute-start.1 = (bf16[160,256]{1,0:T(8,128)(2,1)S(1)}, bf16[160,256]{1,0:T(8,128)(2,1)S(1)}, u32[]{:S(2)}, u32[]{:S(2)}) collective-permute-start(bf16[160,256]{1,0:T(8,128)(2,1)S(1)} %get-tuple-element.34), channel_id=1, source_target_pairs={{384,0},{385,1},{416,32},{417,33},{448,64},{449,65},{480,96},{481,... | collective-permute-start | bytes 245768 | tf_op jit(solution)/shard_map/ppermute | solution.py:206
  35.7 5.4 %collective-permute-done = bf16[160,256]{1,0:T(8,128)(2,1)S(1)} collective-permute-done((bf16[160,256]{1,0:T(8,128)(2,1)S(1)}, bf16[160,256]{1,0:T(8,128)(2,1)S(1)}, u32[]{:S(2)}, u32[]{:S(2)}) %collective-permute-start) | collective-permute-done | bytes 81952 | tf_op jit(solution)/shard_map/ppermute | solution.py:206
  41.1 4.6 %collective-permute-done.1 = bf16[160,256]{1,0:T(8,128)(2,1)S(1)} collective-permute-done((bf16[160,256]{1,0:T(8,128)(2,1)S(1)}, bf16[160,256]{1,0:T(8,128)(2,1)S(1)}, u32[]{:S(2)}, u32[]{:S(2)}) %collective-permute-start.1) | collective-permute-done | bytes 81952 | tf_op jit(solution)/shard_map/ppermute | solution.py:206
  45.7 7.4 %collective-permute-start.3 = (bf16[3,160,256]{2,1,0:T(8,128)(2,1)S(1)}, bf16[3,160,256]{2,1,0:T(8,128)(2,1)S(1)}, u32[]{:S(2)}, u32[]{:S(2)}) collective-permute-start(bf16[3,160,256]{2,1,0:T(8,128)(2,1)S(1)} %pad_maximum_fusion.1.refs_0_), channel_id=1, source_target_pairs={{32,0},{33,1},{64,32},{65,33},{96,64},{97,65},{128,96},{129,97},{1... | collective-permute-start | bytes 737288 | tf_op jit(solution)/shard_map/ppermute | solution.py:206
  53.2 1.9 %collective-permute-start.4 = (bf16[3,160,256]{2,1,0:T(8,128)(2,1)S(1)}, bf16[3,160,256]{2,1,0:T(8,128)(2,1)S(1)}, u32[]{:S(2)}, u32[]{:S(2)}) collective-permute-start(bf16[3,160,256]{2,1,0:T(8,128)(2,1)S(1)} %pad_maximum_fusion.1.refs_0_), channel_id=1, source_target_pairs={{480,0},{481,1},{0,32},{1,33},{32,64},{33,65},{64,96},{65,97},{96,... | collective-permute-start | bytes 737288 | tf_op jit(solution)/shard_map/ppermute | solution.py:206
  55.1 4.1 %collective-permute-start.2 = (bf16[160,256]{1,0:T(8,128)(2,1)S(1)}, bf16[160,256]{1,0:T(8,128)(2,1)S(1)}, u32[]{:S(2)}, u32[]{:S(2)}) collective-permute-start(bf16[160,256]{1,0:T(8,128)(2,1)S(1)} %broadcast_select_fusion), channel_id=1, source_target_pairs={{128,0},{385,1},{160,32},{417,33},{192,64},{449,65},{224,96},{481,... | collective-permute-start | bytes 245768 | tf_op jit(solution)/shard_map/ppermute | solution.py:206
  59.2 0.0 all-to-all-done.1
  59.2 5.8 %shard_map.77 = (f32[4096,128]{1,0:T(8,128)S(1)}, f32[4096,128]{1,0:T(8,128)S(1)}) custom-call(bf16[3,160,256]{2,1,0:T(8,128)(2,1)S(1)} %pad_maximum_fusion.1.refs_0_, bf16[4096,256]{1,0:T(8,128)(2,1)S(1)} %bitcast.42), custom_call_target="tpu_custom_call" | custom-call | tf_op jit(solution)/shard_map/pallas_call | solution.py:157
  65.0 1.3 collective-permute-done.2
  66.4 0.0 collective-permute-done.3.refs_0_
  66.4 0.6 collective-permute-done.4.refs_1_
  67.0 1.9 %collective-permute-start.5 = (bf16[4,160,256]{2,1,0:T(8,128)(2,1)S(1)}, bf16[4,160,256]{2,1,0:T(8,128)(2,1)S(1)}, u32[]{:S(2)}, u32[]{:S(2)}) collective-permute-start(bf16[4,160,256]{2,1,0:T(8,128)(2,1)S(1)} %pad_maximum_fusion), channel_id=1, source_target_pairs={{64,0},{449,1},{96,32},{481,33},{128,64},{1,65},{160,96},{33,97},{... | collective-permute-start | bytes 983048 | tf_op jit(solution)/shard_map/ppermute | solution.py:206
  68.9 4.8 %collective-permute-start.6 = (bf16[1,160,256]{2,1,0:T(8,128)(2,1)S(1)}, bf16[1,160,256]{2,1,0:T(8,128)(2,1)S(1)}, u32[]{:S(2)}, u32[]{:S(2)}) collective-permute-start(bf16[1,160,256]{2,1,0:T(8,128)(2,1)S(1)} %bitcast.46), channel_id=1, source_target_pairs={{32,0},{33,1},{64,32},{65,33},{96,64},{97,65},{128,96},{129,97},{1... | collective-permute-start | bytes 245768 | tf_op jit(solution)/shard_map/ppermute | solution.py:206
  73.7 3.4 %collective-permute-start.7 = (bf16[1,160,256]{2,1,0:T(8,128)(2,1)S(1)}, bf16[1,160,256]{2,1,0:T(8,128)(2,1)S(1)}, u32[]{:S(2)}, u32[]{:S(2)}) collective-permute-start(bf16[1,160,256]{2,1,0:T(8,128)(2,1)S(1)} %bitcast.47), channel_id=1, source_target_pairs={{480,0},{481,1},{0,32},{1,33},{32,64},{33,65},{64,96},{65,97},{96,... | collective-permute-start | bytes 245768 | tf_op jit(solution)/shard_map/ppermute | solution.py:206
  77.1 7.8 %shard_map.78.refs_6_ = f32[4096,128]{1,0:T(8,128)S(1)} custom-call(bf16[3,160,256]{2,1,0:T(8,128)(2,1)S(1)} %collective-permute-done.3.refs_0_, bf16[3,160,256]{2,1,0:T(8,128)(2,1)S(1)} %collective-permute-done.4.refs_1_, bf16[4096,256]{1,0:T(8,128)(2,1)S(1)} %bitcast.43, f32[4096,128]{1,0:T(8,128)S(1)} %get-tuple-element.21.refs_3_.refs_5_, ...), custom_call_target="tpu_custom_call" | custom-call | tf_op jit(solution)/shard_map/pallas_call | solution.py:157
  84.9 0.0 copy-start
  84.9 0.0 copy-start.1
  84.9 0.0 copy-start.3
  84.9 0.0 collective-permute-done.6.refs_2_
  84.9 0.0 collective-permute-done.7.refs_3_
  84.9 0.0 collective-permute-done.5.refs_1_
  85.0 8.6 %shard_map.79 = bf16[32,4,2048]{2,1,0:T(4,128)(2,1)S(1)} custom-call(bf16[1,160,256]{2,1,0:T(8,128)(2,1)S(1)} %bitcast.48, bf16[4,160,256]{2,1,0:T(8,128)(2,1)S(1)} %collective-permute-done.5.refs_1_, bf16[1,160,256]{2,1,0:T(8,128)(2,1)S(1)} %collective-permute-done.6.refs_2_, bf16[1,160,256]{2,1,0:T(8,128)(2,1)S(1)} %collective-permute-done.7.refs_3_, ...), custom_call_target="tpu_custom_call" | custom-call | tf_op jit(solution)/shard_map/pallas_call | solution.py:157
  93.6 17.3 %all_to_all.34 = bf16[32,4,2048]{2,1,0:T(4,128)(2,1)S(1)} all-to-all(bf16[32,4,2048]{2,1,0:T(4,128)(2,1)S(1)} %shard_map.79), channel_id=1, replica_groups=mesh['z'=16,'ylo'=2,'yhi'=2,'x'=4,'core'=2] {'ylo','yhi','x','core'}, dimensions={0} | all-to-all | bytes 1048576 | tf_op jit(solution)/shard_map/all_to_all | solution.py:195
  110.9 0.2 convert_reduce_fusion
  111.1 0.0 copy-done
  111.1 0.0 copy-done.1
  111.1 0.2 multiply_reduce_fusion.2
  111.3 21.5 %all_to_all.35 = f32[32,4,4]{2,1,0:T(4,128)S(1)} all-to-all(f32[32,4,4]{2,1,0:T(4,128)S(1)} %broadcast_in_dim.8), channel_id=1, replica_groups=mesh['z'=16,'ylo'=2,'yhi'=2,'x'=4,'core'=2] {'z','ylo'}, dimensions={0} | all-to-all | bytes 4096 | tf_op jit(solution)/shard_map/all_to_all | solution.py:195
  132.9 0.0 copy-done.3
  132.9 0.7 multiply_add_fusion
  (9 shorter events, 0.2 us)
Async XLA Ops:
  2.0 13.7 %all-to-all-start = ((bf16[4,16,128]{2,0,1:T(4,128)(2,1)}), bf16[4,16,128]{2,0,1:T(4,128)(2,1)S(1)}, u32[]{:S(2)}, u32[]{:S(2)}) async-start(bf16[4,16,128]{2,0,1:T(4,128)(2,1)} %convert_bitcast_fusion), calls=%async_computation | async-start | bytes 32768 | tf_op jit(solution)/shard_map/all_to_all | solution.py:233
  15.7 7.1 %copy-start.2 = (bf16[128,256]{1,0:T(8,128)(2,1)S(1)}, bf16[128,256]{1,0:T(8,128)(2,1)}, u32[]{:S(2)}) copy-start(bf16[128,256]{1,0:T(8,128)(2,1)} %get-tuple-element.14) | copy-start | bytes 196612
  15.7 43.5 %all-to-all-start.1 = ((bf16[32,128,256]{2,1,0:T(8,128)(2,1)}), bf16[32,128,256]{2,1,0:T(8,128)(2,1)S(1)}, u32[]{:S(2)}, u32[]{:S(2)}) async-start(bf16[32,128,256]{2,1,0:T(8,128)(2,1)} %get-tuple-element.17), calls=%async_computation.1 | async-start | bytes 4194304 | tf_op jit(solution)/shard_map/all_to_all | solution.py:195
  22.8 18.3 %collective-permute-start = (bf16[160,256]{1,0:T(8,128)(2,1)S(1)}, bf16[160,256]{1,0:T(8,128)(2,1)S(1)}, u32[]{:S(2)}, u32[]{:S(2)}) collective-permute-start(bf16[160,256]{1,0:T(8,128)(2,1)S(1)} %get-tuple-element.34), channel_id=1, source_target_pairs={{128,0},{129,1},{160,32},{161,33},{192,64},{193,65},{224,96},{225,... | collective-permute-start | bytes 245768 | tf_op jit(solution)/shard_map/ppermute | solution.py:206
  33.8 11.9 %collective-permute-start.1 = (bf16[160,256]{1,0:T(8,128)(2,1)S(1)}, bf16[160,256]{1,0:T(8,128)(2,1)S(1)}, u32[]{:S(2)}, u32[]{:S(2)}) collective-permute-start(bf16[160,256]{1,0:T(8,128)(2,1)S(1)} %get-tuple-element.34), channel_id=1, source_target_pairs={{384,0},{385,1},{416,32},{417,33},{448,64},{449,65},{480,96},{481,... | collective-permute-start | bytes 245768 | tf_op jit(solution)/shard_map/ppermute | solution.py:206
  45.7 20.6 %collective-permute-start.3 = (bf16[3,160,256]{2,1,0:T(8,128)(2,1)S(1)}, bf16[3,160,256]{2,1,0:T(8,128)(2,1)S(1)}, u32[]{:S(2)}, u32[]{:S(2)}) collective-permute-start(bf16[3,160,256]{2,1,0:T(8,128)(2,1)S(1)} %pad_maximum_fusion.1.refs_0_), channel_id=1, source_target_pairs={{32,0},{33,1},{64,32},{65,33},{96,64},{97,65},{128,96},{129,97},{1... | collective-permute-start | bytes 737288 | tf_op jit(solution)/shard_map/ppermute | solution.py:206
  53.2 13.8 %collective-permute-start.4 = (bf16[3,160,256]{2,1,0:T(8,128)(2,1)S(1)}, bf16[3,160,256]{2,1,0:T(8,128)(2,1)S(1)}, u32[]{:S(2)}, u32[]{:S(2)}) collective-permute-start(bf16[3,160,256]{2,1,0:T(8,128)(2,1)S(1)} %pad_maximum_fusion.1.refs_0_), channel_id=1, source_target_pairs={{480,0},{481,1},{0,32},{1,33},{32,64},{33,65},{64,96},{65,97},{96,... | collective-permute-start | bytes 737288 | tf_op jit(solution)/shard_map/ppermute | solution.py:206
  55.1 11.2 %collective-permute-start.2 = (bf16[160,256]{1,0:T(8,128)(2,1)S(1)}, bf16[160,256]{1,0:T(8,128)(2,1)S(1)}, u32[]{:S(2)}, u32[]{:S(2)}) collective-permute-start(bf16[160,256]{1,0:T(8,128)(2,1)S(1)} %broadcast_select_fusion), channel_id=1, source_target_pairs={{128,0},{385,1},{160,32},{417,33},{192,64},{449,65},{224,96},{481,... | collective-permute-start | bytes 245768 | tf_op jit(solution)/shard_map/ppermute | solution.py:206
  67.0 18.0 %collective-permute-start.5 = (bf16[4,160,256]{2,1,0:T(8,128)(2,1)S(1)}, bf16[4,160,256]{2,1,0:T(8,128)(2,1)S(1)}, u32[]{:S(2)}, u32[]{:S(2)}) collective-permute-start(bf16[4,160,256]{2,1,0:T(8,128)(2,1)S(1)} %pad_maximum_fusion), channel_id=1, source_target_pairs={{64,0},{449,1},{96,32},{481,33},{128,64},{1,65},{160,96},{33,97},{... | collective-permute-start | bytes 983048 | tf_op jit(solution)/shard_map/ppermute | solution.py:206
  68.9 16.0 %collective-permute-start.6 = (bf16[1,160,256]{2,1,0:T(8,128)(2,1)S(1)}, bf16[1,160,256]{2,1,0:T(8,128)(2,1)S(1)}, u32[]{:S(2)}, u32[]{:S(2)}) collective-permute-start(bf16[1,160,256]{2,1,0:T(8,128)(2,1)S(1)} %bitcast.46), channel_id=1, source_target_pairs={{32,0},{33,1},{64,32},{65,33},{96,64},{97,65},{128,96},{129,97},{1... | collective-permute-start | bytes 245768 | tf_op jit(solution)/shard_map/ppermute | solution.py:206
  73.7 11.2 %collective-permute-start.7 = (bf16[1,160,256]{2,1,0:T(8,128)(2,1)S(1)}, bf16[1,160,256]{2,1,0:T(8,128)(2,1)S(1)}, u32[]{:S(2)}, u32[]{:S(2)}) collective-permute-start(bf16[1,160,256]{2,1,0:T(8,128)(2,1)S(1)} %bitcast.47), channel_id=1, source_target_pairs={{480,0},{481,1},{0,32},{1,33},{32,64},{33,65},{64,96},{65,97},{96,... | collective-permute-start | bytes 245768 | tf_op jit(solution)/shard_map/ppermute | solution.py:206
  84.9 26.2 %copy-start = (f32[4,2048]{1,0:T(4,128)S(1)}, f32[4,2048]{1,0:T(4,128)}, u32[]{:S(2)}) copy-start(f32[4,2048]{1,0:T(4,128)} %param.9) | copy-start | bytes 98308
  84.9 26.2 %copy-start.1 = (f32[4,2048]{1,0:T(4,128)S(1)}, f32[4,2048]{1,0:T(4,128)}, u32[]{:S(2)}) copy-start(f32[4,2048]{1,0:T(4,128)} %param.8) | copy-start | bytes 98308
  84.9 48.0 %copy-start.3 = (f32[4,2048]{1,0:T(4,128)S(1)}, f32[4,2048]{1,0:T(4,128)}, u32[]{:S(2)}) copy-start(f32[4,2048]{1,0:T(4,128)} %param.7) | copy-start | bytes 98308

commit v4 on v3

--- a/solution.py
+++ b/solution.py
@@ -236,27 +236,26 @@
     packed = jnp.concatenate(
         [own_rows, jnp.concatenate([own_dirs[:half], own_dirs[half:]], axis=1)], axis=0
     )
-    first_core = lax.axis_index("core") == 0
 
     cols = exchanged(plane_copies, PLANE).reshape(-1, FEAT)
 
-    ahead = from_z(packed, 4)
-    behind = from_z(packed, -4)
-    far = jnp.stack([packed, ahead, behind])
-    above = from_z(far, 1)
-    below = from_z(far, -1)
-    opposite = from_z(jnp.where(first_core, ahead, behind), 4, -4)
+    first_side = from_z(packed, 4, -4)
+    other_side = from_z(packed, -4, 4)
+    far = jnp.stack([packed, first_side, other_side])
+    first_near = from_z(far, 1, -1)
+    other_near = from_z(far, -1, 1)
+    opposite = from_z(first_side, 4, -4)
     partial_value, col_norms = first_product([far], cols)
 
-    far, opposite, above, below, partial_value = lax.optimization_barrier(
-        (far, opposite[None], above, below, partial_value)
+    far, opposite, first_near, other_near, partial_value = lax.optimization_barrier(
+        (far, opposite[None], first_near, other_near, partial_value)
     )
     second = from_z(jnp.concatenate([far, opposite]), 2, -2)
-    last_above = from_z(opposite, 1)
-    last_below = from_z(opposite, -1)
-    partial_value = tile_product([above, below], cols, col_norms, partial_value)
+    first_last = from_z(opposite, 1, -1)
+    other_last = from_z(opposite, -1, 1)
+    partial_value = tile_product([first_near, other_near], cols, col_norms, partial_value)
     partial_value = tile_product(
-        [opposite, second, last_above, last_below], cols, col_norms, partial_value, last=True
+        [opposite, second, first_last, other_last], cols, col_norms, partial_value, last=True
     )
     pieces = exchanged(partial_value, PLANE)
     image = jnp.sum(pieces.astype(jnp.float32), axis=0) + noise_var * low_direction.astype(

time: 134 us -> 132 us (0.985)
  waiting for transfers between devices: 17.1 us -> 13.8 us
    ppermute x8, waiting for transfers between devices: 11.9 us -> 8.63 us  [from_z(): return lax.ppermute(shard, ('z', 'core'), pairs)]
  transfers between devices with their start and end apart: 10 -> 10, of which waited for: 5 -> 3; matrix products, arithmetic and copies ran while one was open for 0% -> 0% of each run, Pallas kernels for 12% -> 12%
where the time goes in v4:
time: 132 us; the launch traced here: 131 us
  starting transfers between devices  49.9 us (38%)
  blocking collectives  39.1 us (30%)
  Pallas kernels  24.7 us (19%)
  waiting for transfers between devices  13.8 us (10%)
  other arithmetic  2.63 us (2%)
    all_to_all x2, blocking collectives, exchanged(): return lax.all_to_all(pieces, axes, split_axis=0, concat_axis=0, tiled=True)  39.1 us
    ppermute x8, starting transfers between devices, from_z(): return lax.ppermute(shard, ('z', 'core'), pairs)  36.7 us
    pallas_call x3, Pallas kernels, product_call(): pl.pallas_call(functools.partial(kernel, len(sources)), in_specs=[WHOLE]...  22.3 us
    ppermute x8, waiting for transfers between devices, from_z(): return lax.ppermute(shard, ('z', 'core'), pairs)  8.63 us
    all_to_all x1, starting transfers between devices, exchanged(): return lax.all_to_all(pieces, axes, split_axis=0, concat_axis=0, tiled=True)  7.03 us
    all_to_all x1, starting transfers between devices, shards(): lax.all_to_all(low_direction, PROBE, split_axis=1, concat_axis=0, tiled=T...  6.14 us
    all_to_all x1, waiting for transfers between devices, shards(): lax.all_to_all(low_direction, PROBE, split_axis=1, concat_axis=0, tiled=T...  5.19 us
  transfers between devices with their start and end apart: 10, of which 3 were waited for; matrix products, arithmetic and copies ran while one was open for 0% of the time, Pallas kernels for 12%

profile of v4, /device:TPU:8, one launch (start us, length us, event | category | flops | bytes accessed | tf_op | source)
XLA Modules:
  0.0 131.1 jit_solution(15137915315313955797)
XLA Ops:
  0.6 1.4 %convert_bitcast_fusion = bf16[4,16,128]{2,0,1:T(4,128)(2,1)} fusion(f32[4,2048]{1,0:T(4,128)} %param.9), kind=kLoop, calls=%fused_computation.12 | loop fusion | flops 8192 | bytes 49152 | tf_op jit(solution)/shard_map/all_to_all | solution.py:233
  2.0 6.1 %all-to-all-start = ((bf16[4,16,128]{2,0,1:T(4,128)(2,1)}), bf16[4,16,128]{2,0,1:T(4,128)(2,1)S(1)}, u32[]{:S(2)}, u32[]{:S(2)}) async-start(bf16[4,16,128]{2,0,1:T(4,128)(2,1)} %convert_bitcast_fusion), calls=%async_computation | async-start | bytes 32768 | tf_op jit(solution)/shard_map/all_to_all | solution.py:233
  8.1 2.4 %shard_map.76 = (bf16[128,256]{1,0:T(8,128)(2,1)}, bf16[32,128,256]{2,1,0:T(8,128)(2,1)}) custom-call(bf16[128,256]{1,0:T(8,128)(2,1)} %points_ref.1, f32[1,256]{1,0:T(1,128)} %bitcast.56), custom_call_target="tpu_custom_call" | custom-call | tf_op jit(solution)/shard_map/pallas_call | solution.py:219
  10.5 5.2 %all-to-all-done = bf16[4,16,128]{2,0,1:T(4,128)(2,1)S(1)} async-done(((bf16[4,16,128]{2,0,1:T(4,128)(2,1)}), bf16[4,16,128]{2,0,1:T(4,128)(2,1)S(1)}, u32[]{:S(2)}, u32[]{:S(2)}) %all-to-all-start) | async-done | bytes 16416 | tf_op jit(solution)/shard_map/all_to_all | solution.py:233
  15.7 0.0 copy-start.2
  15.7 7.0 %all-to-all-start.1 = ((bf16[32,128,256]{2,1,0:T(8,128)(2,1)}), bf16[32,128,256]{2,1,0:T(8,128)(2,1)S(1)}, u32[]{:S(2)}, u32[]{:S(2)}) async-start(bf16[32,128,256]{2,1,0:T(8,128)(2,1)} %get-tuple-element.17), calls=%async_computation.1 | async-start | bytes 4194304 | tf_op jit(solution)/shard_map/all_to_all | solution.py:195
  22.8 0.0 copy-done.2
  22.8 11.0 %collective-permute-start = (bf16[160,256]{1,0:T(8,128)(2,1)S(1)}, bf16[160,256]{1,0:T(8,128)(2,1)S(1)}, u32[]{:S(2)}, u32[]{:S(2)}) collective-permute-start(bf16[160,256]{1,0:T(8,128)(2,1)S(1)} %get-tuple-element.34), channel_id=1, source_target_pairs={{128,0},{385,1},{160,32},{417,33},{192,64},{449,65},{224,96},{481,... | collective-permute-start | bytes 245768 | tf_op jit(solution)/shard_map/ppermute | solution.py:206
  33.8 1.9 %collective-permute-start.1 = (bf16[160,256]{1,0:T(8,128)(2,1)S(1)}, bf16[160,256]{1,0:T(8,128)(2,1)S(1)}, u32[]{:S(2)}, u32[]{:S(2)}) collective-permute-start(bf16[160,256]{1,0:T(8,128)(2,1)S(1)} %get-tuple-element.34), channel_id=1, source_target_pairs={{384,0},{129,1},{416,32},{161,33},{448,64},{193,65},{480,96},{225,... | collective-permute-start | bytes 245768 | tf_op jit(solution)/shard_map/ppermute | solution.py:206
  35.7 3.9 %collective-permute-done = bf16[160,256]{1,0:T(8,128)(2,1)S(1)} collective-permute-done((bf16[160,256]{1,0:T(8,128)(2,1)S(1)}, bf16[160,256]{1,0:T(8,128)(2,1)S(1)}, u32[]{:S(2)}, u32[]{:S(2)}) %collective-permute-start) | collective-permute-done | bytes 81952 | tf_op jit(solution)/shard_map/ppermute | solution.py:206
  39.6 4.7 %collective-permute-done.1 = bf16[160,256]{1,0:T(8,128)(2,1)S(1)} collective-permute-done((bf16[160,256]{1,0:T(8,128)(2,1)S(1)}, bf16[160,256]{1,0:T(8,128)(2,1)S(1)}, u32[]{:S(2)}, u32[]{:S(2)}) %collective-permute-start.1) | collective-permute-done | bytes 81952 | tf_op jit(solution)/shard_map/ppermute | solution.py:206
  44.3 5.0 %collective-permute-start.3 = (bf16[3,160,256]{2,1,0:T(8,128)(2,1)S(1)}, bf16[3,160,256]{2,1,0:T(8,128)(2,1)S(1)}, u32[]{:S(2)}, u32[]{:S(2)}) collective-permute-start(bf16[3,160,256]{2,1,0:T(8,128)(2,1)S(1)} %pad_maximum_fusion.1.refs_0_), channel_id=1, source_target_pairs={{32,0},{481,1},{64,32},{1,33},{96,64},{33,65},{128,96},{65,97},{16... | collective-permute-start | bytes 737288 | tf_op jit(solution)/shard_map/ppermute | solution.py:206
  49.4 1.9 %collective-permute-start.4 = (bf16[3,160,256]{2,1,0:T(8,128)(2,1)S(1)}, bf16[3,160,256]{2,1,0:T(8,128)(2,1)S(1)}, u32[]{:S(2)}, u32[]{:S(2)}) collective-permute-start(bf16[3,160,256]{2,1,0:T(8,128)(2,1)S(1)} %pad_maximum_fusion.1.refs_0_), channel_id=1, source_target_pairs={{480,0},{33,1},{0,32},{65,33},{32,64},{97,65},{64,96},{129,97},{96... | collective-permute-start | bytes 737288 | tf_op jit(solution)/shard_map/ppermute | solution.py:206
  51.3 6.9 %collective-permute-start.2 = (bf16[160,256]{1,0:T(8,128)(2,1)S(1)}, bf16[160,256]{1,0:T(8,128)(2,1)S(1)}, u32[]{:S(2)}, u32[]{:S(2)}) collective-permute-start(bf16[160,256]{1,0:T(8,128)(2,1)S(1)} %collective-permute-done), channel_id=1, source_target_pairs={{128,0},{385,1},{160,32},{417,33},{192,64},{449,65},{224,96},{481,... | collective-permute-start | bytes 245768 | tf_op jit(solution)/shard_map/ppermute | solution.py:206
  58.2 0.0 all-to-all-done.1
  58.2 5.8 %shard_map.77 = (f32[4096,128]{1,0:T(8,128)S(1)}, f32[4096,128]{1,0:T(8,128)S(1)}) custom-call(bf16[3,160,256]{2,1,0:T(8,128)(2,1)S(1)} %pad_maximum_fusion.1.refs_0_, bf16[4096,256]{1,0:T(8,128)(2,1)S(1)} %bitcast.42), custom_call_target="tpu_custom_call" | custom-call | tf_op jit(solution)/shard_map/pallas_call | solution.py:157
  64.0 0.0 collective-permute-done.2
  64.1 0.0 collective-permute-done.3.refs_0_
  64.1 0.0 collective-permute-done.4.refs_1_
  64.1 4.2 %collective-permute-start.5 = (bf16[4,160,256]{2,1,0:T(8,128)(2,1)S(1)}, bf16[4,160,256]{2,1,0:T(8,128)(2,1)S(1)}, u32[]{:S(2)}, u32[]{:S(2)}) collective-permute-start(bf16[4,160,256]{2,1,0:T(8,128)(2,1)S(1)} %pad_maximum_fusion), channel_id=1, source_target_pairs={{64,0},{449,1},{96,32},{481,33},{128,64},{1,65},{160,96},{33,97},{... | collective-permute-start | bytes 983048 | tf_op jit(solution)/shard_map/ppermute | solution.py:206
  68.3 2.5 %collective-permute-start.6 = (bf16[1,160,256]{2,1,0:T(8,128)(2,1)S(1)}, bf16[1,160,256]{2,1,0:T(8,128)(2,1)S(1)}, u32[]{:S(2)}, u32[]{:S(2)}) collective-permute-start(bf16[1,160,256]{2,1,0:T(8,128)(2,1)S(1)} %bitcast.46), channel_id=1, source_target_pairs={{32,0},{481,1},{64,32},{1,33},{96,64},{33,65},{128,96},{65,97},{16... | collective-permute-start | bytes 245768 | tf_op jit(solution)/shard_map/ppermute | solution.py:206
  70.9 3.3 %collective-permute-start.7 = (bf16[1,160,256]{2,1,0:T(8,128)(2,1)S(1)}, bf16[1,160,256]{2,1,0:T(8,128)(2,1)S(1)}, u32[]{:S(2)}, u32[]{:S(2)}) collective-permute-start(bf16[1,160,256]{2,1,0:T(8,128)(2,1)S(1)} %bitcast.47), channel_id=1, source_target_pairs={{480,0},{33,1},{0,32},{65,33},{32,64},{97,65},{64,96},{129,97},{96... | collective-permute-start | bytes 245768 | tf_op jit(solution)/shard_map/ppermute | solution.py:206
  74.2 7.8 %shard_map.78.refs_6_ = f32[4096,128]{1,0:T(8,128)S(1)} custom-call(bf16[3,160,256]{2,1,0:T(8,128)(2,1)S(1)} %collective-permute-done.3.refs_0_, bf16[3,160,256]{2,1,0:T(8,128)(2,1)S(1)} %collective-permute-done.4.refs_1_, bf16[4096,256]{1,0:T(8,128)(2,1)S(1)} %bitcast.43, f32[4096,128]{1,0:T(8,128)S(1)} %get-tuple-element.21.refs_3_.refs_5_, ...), custom_call_target="tpu_custom_call" | custom-call | tf_op jit(solution)/shard_map/pallas_call | solution.py:157
  82.0 0.0 copy-start
  82.0 0.0 copy-start.1
  82.0 0.0 copy-start.3
  82.0 0.0 collective-permute-done.6.refs_2_
  82.1 0.0 collective-permute-done.7.refs_3_
  82.1 0.0 collective-permute-done.5.refs_1_
  82.1 8.6 %shard_map.79 = bf16[32,4,2048]{2,1,0:T(4,128)(2,1)S(1)} custom-call(bf16[1,160,256]{2,1,0:T(8,128)(2,1)S(1)} %bitcast.48, bf16[4,160,256]{2,1,0:T(8,128)(2,1)S(1)} %collective-permute-done.5.refs_1_, bf16[1,160,256]{2,1,0:T(8,128)(2,1)S(1)} %collective-permute-done.6.refs_2_, bf16[1,160,256]{2,1,0:T(8,128)(2,1)S(1)} %collective-permute-done.7.refs_3_, ...), custom_call_target="tpu_custom_call" | custom-call | tf_op jit(solution)/shard_map/pallas_call | solution.py:157
  90.7 17.3 %all_to_all.34 = bf16[32,4,2048]{2,1,0:T(4,128)(2,1)S(1)} all-to-all(bf16[32,4,2048]{2,1,0:T(4,128)(2,1)S(1)} %shard_map.79), channel_id=1, replica_groups=mesh['z'=16,'ylo'=2,'yhi'=2,'x'=4,'core'=2] {'ylo','yhi','x','core'}, dimensions={0} | all-to-all | bytes 1048576 | tf_op jit(solution)/shard_map/all_to_all | solution.py:195
  108.0 0.2 convert_reduce_fusion
  108.2 0.0 copy-done
  108.2 0.0 copy-done.1
  108.2 0.2 multiply_reduce_fusion.2
  108.4 21.9 %all_to_all.35 = f32[32,4,4]{2,1,0:T(4,128)S(1)} all-to-all(f32[32,4,4]{2,1,0:T(4,128)S(1)} %broadcast_in_dim.8), channel_id=1, replica_groups=mesh['z'=16,'ylo'=2,'yhi'=2,'x'=4,'core'=2] {'z','ylo'}, dimensions={0} | all-to-all | bytes 4096 | tf_op jit(solution)/shard_map/all_to_all | solution.py:195
  130.4 0.0 copy-done.3
  130.4 0.7 multiply_add_fusion
  (8 shorter events, 0.2 us)
Async XLA Ops:
  2.0 13.7 %all-to-all-start = ((bf16[4,16,128]{2,0,1:T(4,128)(2,1)}), bf16[4,16,128]{2,0,1:T(4,128)(2,1)S(1)}, u32[]{:S(2)}, u32[]{:S(2)}) async-start(bf16[4,16,128]{2,0,1:T(4,128)(2,1)} %convert_bitcast_fusion), calls=%async_computation | async-start | bytes 32768 | tf_op jit(solution)/shard_map/all_to_all | solution.py:233
  15.7 7.1 %copy-start.2 = (bf16[128,256]{1,0:T(8,128)(2,1)S(1)}, bf16[128,256]{1,0:T(8,128)(2,1)}, u32[]{:S(2)}) copy-start(bf16[128,256]{1,0:T(8,128)(2,1)} %get-tuple-element.14) | copy-start | bytes 196612
  15.7 42.5 %all-to-all-start.1 = ((bf16[32,128,256]{2,1,0:T(8,128)(2,1)}), bf16[32,128,256]{2,1,0:T(8,128)(2,1)S(1)}, u32[]{:S(2)}, u32[]{:S(2)}) async-start(bf16[32,128,256]{2,1,0:T(8,128)(2,1)} %get-tuple-element.17), calls=%async_computation.1 | async-start | bytes 4194304 | tf_op jit(solution)/shard_map/all_to_all | solution.py:195
  22.8 16.8 %collective-permute-start = (bf16[160,256]{1,0:T(8,128)(2,1)S(1)}, bf16[160,256]{1,0:T(8,128)(2,1)S(1)}, u32[]{:S(2)}, u32[]{:S(2)}) collective-permute-start(bf16[160,256]{1,0:T(8,128)(2,1)S(1)} %get-tuple-element.34), channel_id=1, source_target_pairs={{128,0},{385,1},{160,32},{417,33},{192,64},{449,65},{224,96},{481,... | collective-permute-start | bytes 245768 | tf_op jit(solution)/shard_map/ppermute | solution.py:206
  33.8 10.5 %collective-permute-start.1 = (bf16[160,256]{1,0:T(8,128)(2,1)S(1)}, bf16[160,256]{1,0:T(8,128)(2,1)S(1)}, u32[]{:S(2)}, u32[]{:S(2)}) collective-permute-start(bf16[160,256]{1,0:T(8,128)(2,1)S(1)} %get-tuple-element.34), channel_id=1, source_target_pairs={{384,0},{129,1},{416,32},{161,33},{448,64},{193,65},{480,96},{225,... | collective-permute-start | bytes 245768 | tf_op jit(solution)/shard_map/ppermute | solution.py:206
  44.3 19.7 %collective-permute-start.3 = (bf16[3,160,256]{2,1,0:T(8,128)(2,1)S(1)}, bf16[3,160,256]{2,1,0:T(8,128)(2,1)S(1)}, u32[]{:S(2)}, u32[]{:S(2)}) collective-permute-start(bf16[3,160,256]{2,1,0:T(8,128)(2,1)S(1)} %pad_maximum_fusion.1.refs_0_), channel_id=1, source_target_pairs={{32,0},{481,1},{64,32},{1,33},{96,64},{33,65},{128,96},{65,97},{16... | collective-permute-start | bytes 737288 | tf_op jit(solution)/shard_map/ppermute | solution.py:206
  49.4 14.7 %collective-permute-start.4 = (bf16[3,160,256]{2,1,0:T(8,128)(2,1)S(1)}, bf16[3,160,256]{2,1,0:T(8,128)(2,1)S(1)}, u32[]{:S(2)}, u32[]{:S(2)}) collective-permute-start(bf16[3,160,256]{2,1,0:T(8,128)(2,1)S(1)} %pad_maximum_fusion.1.refs_0_), channel_id=1, source_target_pairs={{480,0},{33,1},{0,32},{65,33},{32,64},{97,65},{64,96},{129,97},{96... | collective-permute-start | bytes 737288 | tf_op jit(solution)/shard_map/ppermute | solution.py:206
  51.3 12.8 %collective-permute-start.2 = (bf16[160,256]{1,0:T(8,128)(2,1)S(1)}, bf16[160,256]{1,0:T(8,128)(2,1)S(1)}, u32[]{:S(2)}, u32[]{:S(2)}) collective-permute-start(bf16[160,256]{1,0:T(8,128)(2,1)S(1)} %collective-permute-done), channel_id=1, source_target_pairs={{128,0},{385,1},{160,32},{417,33},{192,64},{449,65},{224,96},{481,... | collective-permute-start | bytes 245768 | tf_op jit(solution)/shard_map/ppermute | solution.py:206
  64.1 18.0 %collective-permute-start.5 = (bf16[4,160,256]{2,1,0:T(8,128)(2,1)S(1)}, bf16[4,160,256]{2,1,0:T(8,128)(2,1)S(1)}, u32[]{:S(2)}, u32[]{:S(2)}) collective-permute-start(bf16[4,160,256]{2,1,0:T(8,128)(2,1)S(1)} %pad_maximum_fusion), channel_id=1, source_target_pairs={{64,0},{449,1},{96,32},{481,33},{128,64},{1,65},{160,96},{33,97},{... | collective-permute-start | bytes 983048 | tf_op jit(solution)/shard_map/ppermute | solution.py:206
  68.3 13.7 %collective-permute-start.6 = (bf16[1,160,256]{2,1,0:T(8,128)(2,1)S(1)}, bf16[1,160,256]{2,1,0:T(8,128)(2,1)S(1)}, u32[]{:S(2)}, u32[]{:S(2)}) collective-permute-start(bf16[1,160,256]{2,1,0:T(8,128)(2,1)S(1)} %bitcast.46), channel_id=1, source_target_pairs={{32,0},{481,1},{64,32},{1,33},{96,64},{33,65},{128,96},{65,97},{16... | collective-permute-start | bytes 245768 | tf_op jit(solution)/shard_map/ppermute | solution.py:206
  70.9 11.2 %collective-permute-start.7 = (bf16[1,160,256]{2,1,0:T(8,128)(2,1)S(1)}, bf16[1,160,256]{2,1,0:T(8,128)(2,1)S(1)}, u32[]{:S(2)}, u32[]{:S(2)}) collective-permute-start(bf16[1,160,256]{2,1,0:T(8,128)(2,1)S(1)} %bitcast.47), channel_id=1, source_target_pairs={{480,0},{33,1},{0,32},{65,33},{32,64},{97,65},{64,96},{129,97},{96... | collective-permute-start | bytes 245768 | tf_op jit(solution)/shard_map/ppermute | solution.py:206
  82.0 26.2 %copy-start = (f32[4,2048]{1,0:T(4,128)S(1)}, f32[4,2048]{1,0:T(4,128)}, u32[]{:S(2)}) copy-start(f32[4,2048]{1,0:T(4,128)} %param.9) | copy-start | bytes 98308
  82.0 26.2 %copy-start.1 = (f32[4,2048]{1,0:T(4,128)S(1)}, f32[4,2048]{1,0:T(4,128)}, u32[]{:S(2)}) copy-start(f32[4,2048]{1,0:T(4,128)} %param.8) | copy-start | bytes 98308
  82.0 48.3 %copy-start.3 = (f32[4,2048]{1,0:T(4,128)S(1)}, f32[4,2048]{1,0:T(4,128)}, u32[]{:S(2)}) copy-start(f32[4,2048]{1,0:T(4,128)} %param.7) | copy-start | bytes 98308

commit v5 on v4

--- a/solution.py
+++ b/solution.py
@@ -250,7 +250,7 @@
     far, opposite, first_near, other_near, partial_value = lax.optimization_barrier(
         (far, opposite[None], first_near, other_near, partial_value)
     )
-    second = from_z(jnp.concatenate([far, opposite]), 2, -2)
+    second = from_z(jnp.concatenate([far, opposite]), -2, 2)
     first_last = from_z(opposite, 1, -1)
     other_last = from_z(opposite, -1, 1)
     partial_value = tile_product([first_near, other_near], cols, col_norms, partial_value)

time: 132 us -> 132 us (level)
  no operation moved by 1% of the time
where the time goes in v5:
time: 132 us; the launch traced here: 131 us
  starting transfers between devices  48.6 us (37%)
  blocking collectives  40.3 us (31%)
  Pallas kernels  24.7 us (19%)
  waiting for transfers between devices  13.8 us (10%)
  other arithmetic  2.63 us (2%)
    all_to_all x2, blocking collectives, exchanged(): return lax.all_to_all(pieces, axes, split_axis=0, concat_axis=0, tiled=True)  40.3 us
    ppermute x8, starting transfers between devices, from_z(): return lax.ppermute(shard, ('z', 'core'), pairs)  35.4 us
    pallas_call x3, Pallas kernels, product_call(): pl.pallas_call(functools.partial(kernel, len(sources)), in_specs=[WHOLE]...  22.3 us
    ppermute x8, waiting for transfers between devices, from_z(): return lax.ppermute(shard, ('z', 'core'), pairs)  8.63 us
    all_to_all x1, starting transfers between devices, exchanged(): return lax.all_to_all(pieces, axes, split_axis=0, concat_axis=0, tiled=True)  7.03 us
    all_to_all x1, starting transfers between devices, shards(): lax.all_to_all(low_direction, PROBE, split_axis=1, concat_axis=0, tiled=T...  6.14 us
    all_to_all x1, waiting for transfers between devices, shards(): lax.all_to_all(low_direction, PROBE, split_axis=1, concat_axis=0, tiled=T...  5.19 us
  transfers between devices with their start and end apart: 10, of which 3 were waited for; matrix products, arithmetic and copies ran while one was open for 0% of the time, Pallas kernels for 12%

profile of v5, /device:TPU:8, one launch (start us, length us, event | category | flops | bytes accessed | tf_op | source)
XLA Modules:
  0.0 130.9 jit_solution(4965678882078180497)
XLA Ops:
  0.6 1.4 %convert_bitcast_fusion = bf16[4,16,128]{2,0,1:T(4,128)(2,1)} fusion(f32[4,2048]{1,0:T(4,128)} %param.9), kind=kLoop, calls=%fused_computation.12 | loop fusion | flops 8192 | bytes 49152 | tf_op jit(solution)/shard_map/all_to_all | solution.py:233
  2.0 6.1 %all-to-all-start = ((bf16[4,16,128]{2,0,1:T(4,128)(2,1)}), bf16[4,16,128]{2,0,1:T(4,128)(2,1)S(1)}, u32[]{:S(2)}, u32[]{:S(2)}) async-start(bf16[4,16,128]{2,0,1:T(4,128)(2,1)} %convert_bitcast_fusion), calls=%async_computation | async-start | bytes 32768 | tf_op jit(solution)/shard_map/all_to_all | solution.py:233
  8.1 2.4 %shard_map.76 = (bf16[128,256]{1,0:T(8,128)(2,1)}, bf16[32,128,256]{2,1,0:T(8,128)(2,1)}) custom-call(bf16[128,256]{1,0:T(8,128)(2,1)} %points_ref.1, f32[1,256]{1,0:T(1,128)} %bitcast.56), custom_call_target="tpu_custom_call" | custom-call | tf_op jit(solution)/shard_map/pallas_call | solution.py:219
  10.5 5.2 %all-to-all-done = bf16[4,16,128]{2,0,1:T(4,128)(2,1)S(1)} async-done(((bf16[4,16,128]{2,0,1:T(4,128)(2,1)}), bf16[4,16,128]{2,0,1:T(4,128)(2,1)S(1)}, u32[]{:S(2)}, u32[]{:S(2)}) %all-to-all-start) | async-done | bytes 16416 | tf_op jit(solution)/shard_map/all_to_all | solution.py:233
  15.7 0.0 copy-start.2
  15.7 7.0 %all-to-all-start.1 = ((bf16[32,128,256]{2,1,0:T(8,128)(2,1)}), bf16[32,128,256]{2,1,0:T(8,128)(2,1)S(1)}, u32[]{:S(2)}, u32[]{:S(2)}) async-start(bf16[32,128,256]{2,1,0:T(8,128)(2,1)} %get-tuple-element.17), calls=%async_computation.1 | async-start | bytes 4194304 | tf_op jit(solution)/shard_map/all_to_all | solution.py:195
  22.8 0.0 copy-done.2
  22.8 11.0 %collective-permute-start = (bf16[160,256]{1,0:T(8,128)(2,1)S(1)}, bf16[160,256]{1,0:T(8,128)(2,1)S(1)}, u32[]{:S(2)}, u32[]{:S(2)}) collective-permute-start(bf16[160,256]{1,0:T(8,128)(2,1)S(1)} %get-tuple-element.34), channel_id=1, source_target_pairs={{128,0},{385,1},{160,32},{417,33},{192,64},{449,65},{224,96},{481,... | collective-permute-start | bytes 245768 | tf_op jit(solution)/shard_map/ppermute | solution.py:206
  33.8 1.9 %collective-permute-start.1 = (bf16[160,256]{1,0:T(8,128)(2,1)S(1)}, bf16[160,256]{1,0:T(8,128)(2,1)S(1)}, u32[]{:S(2)}, u32[]{:S(2)}) collective-permute-start(bf16[160,256]{1,0:T(8,128)(2,1)S(1)} %get-tuple-element.34), channel_id=1, source_target_pairs={{384,0},{129,1},{416,32},{161,33},{448,64},{193,65},{480,96},{225,... | collective-permute-start | bytes 245768 | tf_op jit(solution)/shard_map/ppermute | solution.py:206
  35.7 3.9 %collective-permute-done = bf16[160,256]{1,0:T(8,128)(2,1)S(1)} collective-permute-done((bf16[160,256]{1,0:T(8,128)(2,1)S(1)}, bf16[160,256]{1,0:T(8,128)(2,1)S(1)}, u32[]{:S(2)}, u32[]{:S(2)}) %collective-permute-start) | collective-permute-done | bytes 81952 | tf_op jit(solution)/shard_map/ppermute | solution.py:206
  39.6 4.7 %collective-permute-done.1 = bf16[160,256]{1,0:T(8,128)(2,1)S(1)} collective-permute-done((bf16[160,256]{1,0:T(8,128)(2,1)S(1)}, bf16[160,256]{1,0:T(8,128)(2,1)S(1)}, u32[]{:S(2)}, u32[]{:S(2)}) %collective-permute-start.1) | collective-permute-done | bytes 81952 | tf_op jit(solution)/shard_map/ppermute | solution.py:206
  44.3 5.0 %collective-permute-start.3 = (bf16[3,160,256]{2,1,0:T(8,128)(2,1)S(1)}, bf16[3,160,256]{2,1,0:T(8,128)(2,1)S(1)}, u32[]{:S(2)}, u32[]{:S(2)}) collective-permute-start(bf16[3,160,256]{2,1,0:T(8,128)(2,1)S(1)} %pad_maximum_fusion.1.refs_0_), channel_id=1, source_target_pairs={{32,0},{481,1},{64,32},{1,33},{96,64},{33,65},{128,96},{65,97},{16... | collective-permute-start | bytes 737288 | tf_op jit(solution)/shard_map/ppermute | solution.py:206
  49.4 1.9 %collective-permute-start.4 = (bf16[3,160,256]{2,1,0:T(8,128)(2,1)S(1)}, bf16[3,160,256]{2,1,0:T(8,128)(2,1)S(1)}, u32[]{:S(2)}, u32[]{:S(2)}) collective-permute-start(bf16[3,160,256]{2,1,0:T(8,128)(2,1)S(1)} %pad_maximum_fusion.1.refs_0_), channel_id=1, source_target_pairs={{480,0},{33,1},{0,32},{65,33},{32,64},{97,65},{64,96},{129,97},{96... | collective-permute-start | bytes 737288 | tf_op jit(solution)/shard_map/ppermute | solution.py:206
  51.3 6.9 %collective-permute-start.2 = (bf16[160,256]{1,0:T(8,128)(2,1)S(1)}, bf16[160,256]{1,0:T(8,128)(2,1)S(1)}, u32[]{:S(2)}, u32[]{:S(2)}) collective-permute-start(bf16[160,256]{1,0:T(8,128)(2,1)S(1)} %collective-permute-done), channel_id=1, source_target_pairs={{128,0},{385,1},{160,32},{417,33},{192,64},{449,65},{224,96},{481,... | collective-permute-start | bytes 245768 | tf_op jit(solution)/shard_map/ppermute | solution.py:206
  58.2 0.0 all-to-all-done.1
  58.2 5.8 %shard_map.77 = (f32[4096,128]{1,0:T(8,128)S(1)}, f32[4096,128]{1,0:T(8,128)S(1)}) custom-call(bf16[3,160,256]{2,1,0:T(8,128)(2,1)S(1)} %pad_maximum_fusion.1.refs_0_, bf16[4096,256]{1,0:T(8,128)(2,1)S(1)} %bitcast.42), custom_call_target="tpu_custom_call" | custom-call | tf_op jit(solution)/shard_map/pallas_call | solution.py:157
  64.0 0.0 collective-permute-done.2
  64.1 0.0 collective-permute-done.3.refs_0_
  64.1 0.0 collective-permute-done.4.refs_1_
  64.1 2.2 %collective-permute-start.5 = (bf16[4,160,256]{2,1,0:T(8,128)(2,1)S(1)}, bf16[4,160,256]{2,1,0:T(8,128)(2,1)S(1)}, u32[]{:S(2)}, u32[]{:S(2)}) collective-permute-start(bf16[4,160,256]{2,1,0:T(8,128)(2,1)S(1)} %pad_maximum_fusion), channel_id=1, source_target_pairs={{448,0},{65,1},{480,32},{97,33},{0,64},{129,65},{32,96},{161,97},{... | collective-permute-start | bytes 983048 | tf_op jit(solution)/shard_map/ppermute | solution.py:206
  66.4 4.5 %collective-permute-start.6 = (bf16[1,160,256]{2,1,0:T(8,128)(2,1)S(1)}, bf16[1,160,256]{2,1,0:T(8,128)(2,1)S(1)}, u32[]{:S(2)}, u32[]{:S(2)}) collective-permute-start(bf16[1,160,256]{2,1,0:T(8,128)(2,1)S(1)} %bitcast.46), channel_id=1, source_target_pairs={{32,0},{481,1},{64,32},{1,33},{96,64},{33,65},{128,96},{65,97},{16... | collective-permute-start | bytes 245768 | tf_op jit(solution)/shard_map/ppermute | solution.py:206
  70.8 2.1 %collective-permute-start.7 = (bf16[1,160,256]{2,1,0:T(8,128)(2,1)S(1)}, bf16[1,160,256]{2,1,0:T(8,128)(2,1)S(1)}, u32[]{:S(2)}, u32[]{:S(2)}) collective-permute-start(bf16[1,160,256]{2,1,0:T(8,128)(2,1)S(1)} %bitcast.47), channel_id=1, source_target_pairs={{480,0},{33,1},{0,32},{65,33},{32,64},{97,65},{64,96},{129,97},{96... | collective-permute-start | bytes 245768 | tf_op jit(solution)/shard_map/ppermute | solution.py:206
  72.9 7.8 %shard_map.78.refs_6_ = f32[4096,128]{1,0:T(8,128)S(1)} custom-call(bf16[3,160,256]{2,1,0:T(8,128)(2,1)S(1)} %collective-permute-done.3.refs_0_, bf16[3,160,256]{2,1,0:T(8,128)(2,1)S(1)} %collective-permute-done.4.refs_1_, bf16[4096,256]{1,0:T(8,128)(2,1)S(1)} %bitcast.43, f32[4096,128]{1,0:T(8,128)S(1)} %get-tuple-element.21.refs_3_.refs_5_, ...), custom_call_target="tpu_custom_call" | custom-call | tf_op jit(solution)/shard_map/pallas_call | solution.py:157
  80.7 0.0 copy-start
  80.7 0.0 copy-start.1
  80.7 0.0 copy-start.3
  80.7 0.0 collective-permute-done.6.refs_2_
  80.7 0.0 collective-permute-done.7.refs_3_
  80.8 0.0 collective-permute-done.5.refs_1_
  80.8 8.6 %shard_map.79 = bf16[32,4,2048]{2,1,0:T(4,128)(2,1)S(1)} custom-call(bf16[1,160,256]{2,1,0:T(8,128)(2,1)S(1)} %bitcast.48, bf16[4,160,256]{2,1,0:T(8,128)(2,1)S(1)} %collective-permute-done.5.refs_1_, bf16[1,160,256]{2,1,0:T(8,128)(2,1)S(1)} %collective-permute-done.6.refs_2_, bf16[1,160,256]{2,1,0:T(8,128)(2,1)S(1)} %collective-permute-done.7.refs_3_, ...), custom_call_target="tpu_custom_call" | custom-call | tf_op jit(solution)/shard_map/pallas_call | solution.py:157
  89.4 17.3 %all_to_all.34 = bf16[32,4,2048]{2,1,0:T(4,128)(2,1)S(1)} all-to-all(bf16[32,4,2048]{2,1,0:T(4,128)(2,1)S(1)} %shard_map.79), channel_id=1, replica_groups=mesh['z'=16,'ylo'=2,'yhi'=2,'x'=4,'core'=2] {'ylo','yhi','x','core'}, dimensions={0} | all-to-all | bytes 1048576 | tf_op jit(solution)/shard_map/all_to_all | solution.py:195
  106.7 0.2 convert_reduce_fusion
  106.9 0.0 copy-done
  106.9 0.0 copy-done.1
  106.9 0.2 multiply_reduce_fusion.2
  107.1 23.0 %all_to_all.35 = f32[32,4,4]{2,1,0:T(4,128)S(1)} all-to-all(f32[32,4,4]{2,1,0:T(4,128)S(1)} %broadcast_in_dim.8), channel_id=1, replica_groups=mesh['z'=16,'ylo'=2,'yhi'=2,'x'=4,'core'=2] {'z','ylo'}, dimensions={0} | all-to-all | bytes 4096 | tf_op jit(solution)/shard_map/all_to_all | solution.py:195
  130.2 0.0 copy-done.3
  130.2 0.7 multiply_add_fusion
  (8 shorter events, 0.2 us)
Async XLA Ops:
  2.0 13.7 %all-to-all-start = ((bf16[4,16,128]{2,0,1:T(4,128)(2,1)}), bf16[4,16,128]{2,0,1:T(4,128)(2,1)S(1)}, u32[]{:S(2)}, u32[]{:S(2)}) async-start(bf16[4,16,128]{2,0,1:T(4,128)(2,1)} %convert_bitcast_fusion), calls=%async_computation | async-start | bytes 32768 | tf_op jit(solution)/shard_map/all_to_all | solution.py:233
  15.7 7.1 %copy-start.2 = (bf16[128,256]{1,0:T(8,128)(2,1)S(1)}, bf16[128,256]{1,0:T(8,128)(2,1)}, u32[]{:S(2)}) copy-start(bf16[128,256]{1,0:T(8,128)(2,1)} %get-tuple-element.14) | copy-start | bytes 196612
  15.7 42.5 %all-to-all-start.1 = ((bf16[32,128,256]{2,1,0:T(8,128)(2,1)}), bf16[32,128,256]{2,1,0:T(8,128)(2,1)S(1)}, u32[]{:S(2)}, u32[]{:S(2)}) async-start(bf16[32,128,256]{2,1,0:T(8,128)(2,1)} %get-tuple-element.17), calls=%async_computation.1 | async-start | bytes 4194304 | tf_op jit(solution)/shard_map/all_to_all | solution.py:195
  22.8 16.8 %collective-permute-start = (bf16[160,256]{1,0:T(8,128)(2,1)S(1)}, bf16[160,256]{1,0:T(8,128)(2,1)S(1)}, u32[]{:S(2)}, u32[]{:S(2)}) collective-permute-start(bf16[160,256]{1,0:T(8,128)(2,1)S(1)} %get-tuple-element.34), channel_id=1, source_target_pairs={{128,0},{385,1},{160,32},{417,33},{192,64},{449,65},{224,96},{481,... | collective-permute-start | bytes 245768 | tf_op jit(solution)/shard_map/ppermute | solution.py:206
  33.8 10.5 %collective-permute-start.1 = (bf16[160,256]{1,0:T(8,128)(2,1)S(1)}, bf16[160,256]{1,0:T(8,128)(2,1)S(1)}, u32[]{:S(2)}, u32[]{:S(2)}) collective-permute-start(bf16[160,256]{1,0:T(8,128)(2,1)S(1)} %get-tuple-element.34), channel_id=1, source_target_pairs={{384,0},{129,1},{416,32},{161,33},{448,64},{193,65},{480,96},{225,... | collective-permute-start | bytes 245768 | tf_op jit(solution)/shard_map/ppermute | solution.py:206
  44.3 19.7 %collective-permute-start.3 = (bf16[3,160,256]{2,1,0:T(8,128)(2,1)S(1)}, bf16[3,160,256]{2,1,0:T(8,128)(2,1)S(1)}, u32[]{:S(2)}, u32[]{:S(2)}) collective-permute-start(bf16[3,160,256]{2,1,0:T(8,128)(2,1)S(1)} %pad_maximum_fusion.1.refs_0_), channel_id=1, source_target_pairs={{32,0},{481,1},{64,32},{1,33},{96,64},{33,65},{128,96},{65,97},{16... | collective-permute-start | bytes 737288 | tf_op jit(solution)/shard_map/ppermute | solution.py:206
  49.4 14.7 %collective-permute-start.4 = (bf16[3,160,256]{2,1,0:T(8,128)(2,1)S(1)}, bf16[3,160,256]{2,1,0:T(8,128)(2,1)S(1)}, u32[]{:S(2)}, u32[]{:S(2)}) collective-permute-start(bf16[3,160,256]{2,1,0:T(8,128)(2,1)S(1)} %pad_maximum_fusion.1.refs_0_), channel_id=1, source_target_pairs={{480,0},{33,1},{0,32},{65,33},{32,64},{97,65},{64,96},{129,97},{96... | collective-permute-start | bytes 737288 | tf_op jit(solution)/shard_map/ppermute | solution.py:206
  51.3 12.8 %collective-permute-start.2 = (bf16[160,256]{1,0:T(8,128)(2,1)S(1)}, bf16[160,256]{1,0:T(8,128)(2,1)S(1)}, u32[]{:S(2)}, u32[]{:S(2)}) collective-permute-start(bf16[160,256]{1,0:T(8,128)(2,1)S(1)} %collective-permute-done), channel_id=1, source_target_pairs={{128,0},{385,1},{160,32},{417,33},{192,64},{449,65},{224,96},{481,... | collective-permute-start | bytes 245768 | tf_op jit(solution)/shard_map/ppermute | solution.py:206
  64.1 16.6 %collective-permute-start.5 = (bf16[4,160,256]{2,1,0:T(8,128)(2,1)S(1)}, bf16[4,160,256]{2,1,0:T(8,128)(2,1)S(1)}, u32[]{:S(2)}, u32[]{:S(2)}) collective-permute-start(bf16[4,160,256]{2,1,0:T(8,128)(2,1)S(1)} %pad_maximum_fusion), channel_id=1, source_target_pairs={{448,0},{65,1},{480,32},{97,33},{0,64},{129,65},{32,96},{161,97},{... | collective-permute-start | bytes 983048 | tf_op jit(solution)/shard_map/ppermute | solution.py:206
  66.4 14.4 %collective-permute-start.6 = (bf16[1,160,256]{2,1,0:T(8,128)(2,1)S(1)}, bf16[1,160,256]{2,1,0:T(8,128)(2,1)S(1)}, u32[]{:S(2)}, u32[]{:S(2)}) collective-permute-start(bf16[1,160,256]{2,1,0:T(8,128)(2,1)S(1)} %bitcast.46), channel_id=1, source_target_pairs={{32,0},{481,1},{64,32},{1,33},{96,64},{33,65},{128,96},{65,97},{16... | collective-permute-start | bytes 245768 | tf_op jit(solution)/shard_map/ppermute | solution.py:206
  70.8 9.9 %collective-permute-start.7 = (bf16[1,160,256]{2,1,0:T(8,128)(2,1)S(1)}, bf16[1,160,256]{2,1,0:T(8,128)(2,1)S(1)}, u32[]{:S(2)}, u32[]{:S(2)}) collective-permute-start(bf16[1,160,256]{2,1,0:T(8,128)(2,1)S(1)} %bitcast.47), channel_id=1, source_target_pairs={{480,0},{33,1},{0,32},{65,33},{32,64},{97,65},{64,96},{129,97},{96... | collective-permute-start | bytes 245768 | tf_op jit(solution)/shard_map/ppermute | solution.py:206
  80.7 26.2 %copy-start = (f32[4,2048]{1,0:T(4,128)S(1)}, f32[4,2048]{1,0:T(4,128)}, u32[]{:S(2)}) copy-start(f32[4,2048]{1,0:T(4,128)} %param.9) | copy-start | bytes 98308
  80.7 26.2 %copy-start.1 = (f32[4,2048]{1,0:T(4,128)S(1)}, f32[4,2048]{1,0:T(4,128)}, u32[]{:S(2)}) copy-start(f32[4,2048]{1,0:T(4,128)} %param.8) | copy-start | bytes 98308
  80.7 49.5 %copy-start.3 = (f32[4,2048]{1,0:T(4,128)S(1)}, f32[4,2048]{1,0:T(4,128)}, u32[]{:S(2)}) copy-start(f32[4,2048]{1,0:T(4,128)} %param.7) | copy-start | bytes 98308
